TPU v7x, 32 devices: a whole 2x2x4 slice. The times are simulated.
32 devices in a mesh: slab: 8 (over z, y), pair: 4 (over x, core).
Axes of the slice: x: 2, y: 2, z: 4, core: 2. Of those that a mesh axis runs over, the one named last changes fastest.
Arguments:
- initial_warmth: float32 [128, 256, 512], P('slab', 'pair'), may hold values from 0.5 to 1.5
- heat_passing_coefficient: float32 [128, 256, 512], P('slab', 'pair'), may hold values from 0.2 to 2
- mirror_fraction: float32 [512, 128], P(('slab', 'pair')), may hold values from 0.3 to 0.9
- element_facing_site: int32 [512, 128], P(('slab', 'pair')), may hold values from 0 to 1023
- tile_block_couples: int32 [8192, 2], P(('slab', 'pair')), may hold values from 0 to 511, as said below
- active_slot_count: int32 [32], P(('slab', 'pair')), may hold values from 42 to 256, as said below
- view_factor_blocks: float32 [8192, 128, 128], P(('slab', 'pair')), as said below
Outputs:
- radiosity: float32 [512, 128], P(('slab', 'pair'))
- warmed_liner: float32 [128, 256, 512], P('slab', 'pair')
Inputs may be any that keep to these rules, and one draw needn't show every extreme that they name: `tile_block_couples`: each row names two different blocks, and no unordered pair of blocks appears twice in the whole list. A device's slots from its active_slot_count on are not used; in every draw some device has all 256 slots live, and some other device has the fewest allowed. `view_factor_blocks`: entries are nonnegative.
All inputs are finite; a program needn't handle non-finite values.
Results may differ from a plain program's by a relative error of at most 0.0003.
Values sent between devices are 32-bit elements; how exact they have to be, the bound alone decides.
No kernel may reach another device: no remote copies, remote signals or barrier semaphores. Data moves between devices by JAX's collectives and lax.ppermute only.
A program may use at most 192 MiB of HBM per device.

v0:
```python
import functools

import jax
import jax.numpy as jnp
from jax import lax
from jax.experimental import pallas as pl
from jax.experimental.pallas import tpu as pltpu
from jax.sharding import PartitionSpec as P

BLK = 128
SWEEPS = 2
STEPS = 4
HALO = STEPS
ROWS = STEPS
LANES = 128
CHUNK = 16
LAG = 8

step_size = 0.07

NT = (((1,), (1,)), ((), ()))
NN = (((1,), (0,)), ((), ()))


def params(mib):
    return pltpu.CompilerParams(vmem_limit_bytes=mib * 1024 * 1024)


def cost(flops, nbytes):
    return pl.CostEstimate(flops=flops, bytes_accessed=nbytes, transcendentals=0)


def parts_of(x, count):
    out = []
    for _ in range(count - 1):
        part = x.astype(jnp.bfloat16)
        out.append(part)
        x = x - part.astype(jnp.float32)
    out.append(x.astype(jnp.bfloat16))
    return out


class Lagging:
    def __init__(self, depth):
        self.depth = depth
        self.waiting = []

    def add(self, store):
        self.waiting.append(store)
        if len(self.waiting) > self.depth:
            self.waiting.pop(0)()

    def finish(self):
        for store in self.waiting:
            store()
        self.waiting = []


def put(ref, index, value):
    return lambda: ref.__setitem__(index, value)


def emit_kernel(temp_ref, site_ref, mirror_ref, emitted_ref, copies_ref):
    nx, ny, _ = temp_ref.shape
    sheets = nx * ny // LANES
    per = LANES // ny
    lanes = lax.broadcasted_iota(jnp.int32, (LANES, LANES), 1)
    gathered = jnp.zeros((LANES, LANES), jnp.float32)
    for r in range(sheets):
        piece = temp_ref[per * r : per * r + per].reshape(LANES, LANES)
        if r:
            piece = pltpu.roll(piece, r, 1)
        gathered = jnp.where(lanes == r, piece, gathered)
    plane = gathered.T[:sheets]
    for half in range(site_ref.shape[0] // 8):
        rows = pl.ds(half * 8, 8)
        site = site_ref[rows, :]
        lane = site & (LANES - 1)
        sheet = site >> 7
        warmth = jnp.zeros(site.shape, jnp.float32)
        for r in range(sheets):
            line = jnp.broadcast_to(plane[r : r + 1, :], site.shape)
            picked = jnp.take_along_axis(line, lane, axis=1)
            warmth = jnp.where(sheet == r, picked, warmth)
        square = warmth * warmth
        emitted = (1.0 - mirror_ref[rows, :]) * (square * square)
        emitted_ref[rows, :] = emitted
        for d in range(copies_ref.shape[0]):
            copies_ref[d, rows, :] = emitted


def emit(temp, site, mirror, count):
    shape = mirror.shape
    nx, ny, _ = temp.shape
    patch = pl.BlockSpec(shape, lambda i: (0, 0))
    return pl.pallas_call(
        emit_kernel,
        grid=(1,),
        out_shape=(
            jax.ShapeDtypeStruct(shape, jnp.float32),
            jax.ShapeDtypeStruct((count,) + shape, jnp.float32),
        ),
        in_specs=[pl.BlockSpec((nx, ny, LANES), lambda i: (0, 0, 0)), patch, patch],
        out_specs=(patch, pl.BlockSpec((count,) + shape, lambda i: (0, 0, 0))),
        compiler_params=params(64),
        cost_estimate=cost(10_000, 900_000),
        name="emit",
    )(temp, site, mirror)


def tiles_kernel(
    live_ref, pairs_ref, lanes_ref, whole_ref, tiles_ref, out_ref, held, terms, sems
):
    slots = held.shape[0]
    live = live_ref[0]
    chunks = (live + CHUNK - 1) // CHUNK

    def chunk_copy(c):
        span = pl.ds(c * CHUNK, CHUNK)
        return pltpu.make_async_copy(tiles_ref.at[span], held.at[span], sems.at[c])

    @pl.loop(0, chunks)
    def _(c):
        chunk_copy(c).start()

    top = lax.broadcasted_iota(jnp.int32, (8, BLK), 0) == 0

    def split_row(block):
        row = jnp.broadcast_to(whole_ref[pl.ds(block, 1), :], (8, BLK))
        high = row.astype(jnp.bfloat16).astype(jnp.float32)
        return jnp.where(top, high, row - high)

    def vectors(a, b):
        stacked = jnp.concatenate([split_row(a), split_row(b)], axis=0)
        stacked = stacked.astype(jnp.bfloat16)
        return jnp.concatenate([stacked, stacked], axis=1)

    @pl.loop(0, chunks)
    def _(c):
        chunk_copy(c).wait()
        stores = Lagging(4 * CHUNK)
        for u in range(0, CHUNK, 2):
            t = c * CHUNK + u
            high_a, low_a = parts_of(held[t], 2)
            high_b, low_b = parts_of(held[t + 1], 2)
            both = jnp.concatenate(
                [
                    jnp.concatenate([high_a, high_b], axis=1),
                    jnp.concatenate([low_a, low_b], axis=1),
                ],
                axis=0,
            )
            second = lax.dot_general(
                vectors(pairs_ref[0, t], pairs_ref[0, t + 1]),
                both,
                NN,
                preferred_element_type=jnp.float32,
            )
            turned = jnp.concatenate(
                [
                    jnp.concatenate([high_a, low_a], axis=1),
                    jnp.concatenate([high_b, low_b], axis=1),
                ],
                axis=0,
            )
            first = lax.dot_general(
                vectors(pairs_ref[1, t], pairs_ref[1, t + 1]),
                turned,
                NT,
                preferred_element_type=jnp.float32,
            )
            for side, result in ((0, first), (1, second)):
                for v, (top_row, cols) in enumerate(((0, slice(0, BLK)), (8, slice(BLK, 2 * BLK)))):
                    row = result[top_row : top_row + 1, cols] + result[top_row + 1 : top_row + 2, cols]
                    stores.add(put(terms, (side, pl.ds(t + v, 1)), row))
        stores.finish()

    used = lax.broadcasted_iota(jnp.int32, (slots, BLK), 0) < live
    used_lane = lax.broadcasted_iota(jnp.int32, (1, slots), 1) < live
    blocks = out_ref.shape[0]
    group = min(blocks, 512)
    split = []
    for side in range(2):
        masked = jnp.where(used, terms[side], 0.0)
        split.append(jnp.concatenate(parts_of(masked, 2), axis=1))
    for base in range(0, blocks, group):
        rows = lax.broadcasted_iota(jnp.int32, (group, slots), 0) + base
        total = jnp.zeros((group, 2 * BLK), jnp.float32)
        for side in range(2):
            target = jnp.where(used_lane, lanes_ref[side : side + 1, :], -1)
            choose = jnp.where(rows == target, 1.0, 0.0).astype(jnp.bfloat16)
            total = total + jnp.dot(choose, split[side], preferred_element_type=jnp.float32)
        out_ref[base : base + group, :] = total[:, :BLK] + total[:, BLK:]


def tile_terms(whole, couples, live, tiles):
    slots = tiles.shape[0]
    smem = pl.BlockSpec(memory_space=pltpu.SMEM)
    vmem = pl.BlockSpec(memory_space=pltpu.VMEM)
    return pl.pallas_call(
        tiles_kernel,
        out_shape=jax.ShapeDtypeStruct(whole.shape, jnp.float32),
        in_specs=[smem, smem, vmem, vmem, pl.BlockSpec(memory_space=pl.ANY)],
        out_specs=vmem,
        scratch_shapes=[
            pltpu.VMEM(tiles.shape, jnp.float32),
            pltpu.VMEM((2, slots, BLK), jnp.float32),
            pltpu.SemaphoreType.DMA((slots // CHUNK,)),
        ],
        compiler_params=params(64),
        cost_estimate=cost(slots * BLK * BLK * 32, slots * BLK * BLK * 4),
        name="tiles",
    )(live, couples, couples, whole, tiles)


def sum_parts(parts_ref, rows):
    total = parts_ref[0, rows, :]
    for d in range(1, parts_ref.shape[0]):
        total = total + parts_ref[d, rows, :]
    return total


def middle_kernel(parts_ref, emitted_ref, mirror_ref, copies_ref):
    for half in range(emitted_ref.shape[0] // 8):
        rows = pl.ds(half * 8, 8)
        incident = sum_parts(parts_ref, rows)
        radiosity = emitted_ref[rows, :] + mirror_ref[rows, :] * incident
        for d in range(copies_ref.shape[0]):
            copies_ref[d, rows, :] = radiosity


def middle(parts, emitted, mirror):
    return pl.pallas_call(
        middle_kernel,
        out_shape=jax.ShapeDtypeStruct(parts.shape, jnp.float32),
        compiler_params=params(64),
        cost_estimate=cost(100_000, 600_000),
        name="middle",
    )(parts, emitted, mirror)


def last_kernel(scale, parts_ref, emitted_ref, mirror_ref, site_ref, rad_ref, source_ref):
    blocks = emitted_ref.shape[0]
    incident = sum_parts(parts_ref, slice(None))
    emitted = emitted_ref[...]
    mirror = mirror_ref[...]
    rad_ref[...] = emitted + mirror * incident
    absorbed = ((1.0 - mirror) * incident - emitted) * scale
    site = site_ref[...]
    lane = site & (LANES - 1)
    sheet = site >> 7
    sheets = source_ref.shape[1]
    sheet_iota = lax.broadcasted_iota(jnp.int32, (sheets, BLK), 0)
    lane_iota = lax.broadcasted_iota(jnp.int32, (LANES, BLK), 0)
    left = []
    right = []
    for b in range(blocks):
        here = jnp.where(sheet_iota == sheet[b : b + 1, :], absorbed[b : b + 1, :], 0.0)
        left.append(here)
        pick = jnp.where(lane_iota == lane[b : b + 1, :], 1.0, 0.0)
        right.append(pick.astype(jnp.bfloat16))
    left = jnp.concatenate(left, axis=1)
    right = jnp.concatenate(right, axis=1)
    source = jnp.zeros((sheets, LANES), jnp.float32)
    for part in parts_of(left, 3):
        source = source + lax.dot_general(part, right, NT, preferred_element_type=jnp.float32)
    for d in range(source_ref.shape[0]):
        source_ref[d] = source


def last(parts, emitted, mirror, site, cells, count):
    weight = cells / (mirror.shape[0] * BLK * 1.0)
    return pl.pallas_call(
        functools.partial(last_kernel, step_size * weight),
        out_shape=(
            jax.ShapeDtypeStruct(mirror.shape, jnp.float32),
            jax.ShapeDtypeStruct((count, cells // LANES, LANES), jnp.float32),
        ),
        compiler_params=params(64),
        cost_estimate=cost(10_000_000, 600_000),
        name="last",
    )(parts, emitted, mirror, site)


def pack_y_kernel(t0, k0, t7, k7, down_ref, up_ref):
    upper = lax.broadcasted_iota(jnp.int32, down_ref.shape[1:], 0) < ROWS
    for x in range(down_ref.shape[0]):
        down_ref[x] = jnp.where(upper, t0[x], pltpu.roll(k0[x], ROWS, 0))
        up_ref[x] = jnp.where(upper, pltpu.roll(t7[x], ROWS, 0), k7[x])


def pack_y(temp, cond):
    nx, ny, nz = temp.shape
    first = pl.BlockSpec((nx, 8, nz), lambda i: (0, 0, 0))
    final = pl.BlockSpec((nx, 8, nz), lambda i: (0, ny // 8 - 1, 0))
    shape = jax.ShapeDtypeStruct((nx, 8, nz), jnp.float32)
    return pl.pallas_call(
        pack_y_kernel,
        grid=(1,),
        out_shape=(shape, shape),
        in_specs=[first, first, final, final],
        out_specs=(first, first),
        compiler_params=params(64),
        cost_estimate=cost(0, 4 * nx * 8 * nz * 4),
        name="pack_y",
    )(temp, cond, temp, cond)


def pack_x_kernel(first, final, below0, above0, below1, above1, low_ref, high_ref):
    ny, nz = first.shape[1:]
    upper = lax.broadcasted_iota(jnp.int32, (8, nz), 0) < ROWS
    for send, temp, below, above in (
        (low_ref, first, below0, above0),
        (high_ref, final, below1, above1),
    ):
        for p in range(HALO):
            send[p, :ny] = temp[p]
            send[p, ny : ny + 8] = jnp.where(upper, above[p], pltpu.roll(below[p], ROWS, 0))
            send[p, ny + 8 :] = jnp.where(upper, pltpu.roll(above[p], ROWS, 0), below[p])


def pack_x(temp, below, above):
    nx, ny, nz = temp.shape

    def ends(rows):
        return (
            pl.BlockSpec((HALO, rows, nz), lambda i: (0, 0, 0)),
            pl.BlockSpec((HALO, rows, nz), lambda i: (nx // HALO - 1, 0, 0)),
        )

    first, final = ends(ny)
    first_rows, final_rows = ends(8)
    whole = pl.BlockSpec((HALO, ny + 16, nz), lambda i: (0, 0, 0))
    shape = jax.ShapeDtypeStruct((HALO, ny + 16, nz), jnp.float32)
    return pl.pallas_call(
        pack_x_kernel,
        grid=(1,),
        out_shape=(shape, shape),
        in_specs=[first, final, first_rows, first_rows, final_rows, final_rows],
        out_specs=(whole, whole),
        compiler_params=params(64),
        cost_estimate=cost(0, 4 * HALO * (ny + 16) * nz * 4),
        name="pack_x",
    )(temp, temp, below, above, below, above)


def coupling(a, b):
    return jnp.where(jnp.minimum(a, b) > 0.0, (0.5 * step_size) * (a + b), 0.0)


def neighbours():
    slab, pair = lax.axis_index("slab"), lax.axis_index("pair")
    return slab > 0, slab < lax.axis_size("slab") - 1, pair > 0, pair < lax.axis_size("pair") - 1


def lane_tiles(nz):
    return [slice(j * LANES, (j + 1) * LANES) for j in range(nz // LANES)]


def one_step(field, cond, gz, begin, end, target):
    wide, nz = field.shape[1:]
    tiles = wide // 8
    spans = lane_tiles(nz)
    count = len(spans)
    lane = lax.broadcasted_iota(jnp.int32, (8, LANES), 1)
    sub = lax.broadcasted_iota(jnp.int32, (8, LANES), 0)
    _, _, has_below, has_above = neighbours()
    keep_above = (sub < 7) | has_above
    keep_below = (sub < 7) | has_below

    def row_tile(ref, x, t):
        return [ref[x, 8 * t : 8 * t + 8, z] for z in spans]

    def first_rolled(ref, x):
        return [pltpu.roll(v, 7, 0) for v in row_tile(ref, x, 0)]

    def y_flux(t_now, k_now, t_next, k_next):
        return [
            (k_now[j] + k_next[j]) * (t_next[j] - t_now[j]) for j in range(count)
        ]

    def z_change(x, t, t_now, k_now):
        turned = [pltpu.roll(v, LANES - 1, 1) for v in t_now]
        flux = []
        for j, z in enumerate(spans):
            deep = turned[j + 1] if j + 1 < count else 0.0
            deep = jnp.where(lane < LANES - 1, turned[j], deep)
            flux.append(gz[x, 8 * t : 8 * t + 8, z] * (deep - t_now[j]))
        back = [pltpu.roll(f, 1, 1) for f in flux]
        out = []
        for j in range(count):
            low = back[j - 1] if j else (k_now[0] + k_now[0]) * t_now[0]
            out.append(flux[j] - jnp.where(lane > 0, back[j], low))
        return out

    @pl.loop(begin, end)
    def _(x):
        stores = Lagging(LAG)
        final = y_flux(
            row_tile(field, x, tiles - 1),
            row_tile(cond, x, tiles - 1),
            first_rolled(field, x),
            first_rolled(cond, x),
        )
        low_y = [pltpu.roll(f, 1, 0) for f in final]
        t_now, k_now = row_tile(field, x, 0), row_tile(cond, x, 0)
        for t in range(tiles):
            rows = slice(8 * t, 8 * t + 8)
            if t + 1 < tiles:
                t_next, k_next = row_tile(field, x, t + 1), row_tile(cond, x, t + 1)
            else:
                t_next, k_next = first_rolled(field, x), first_rolled(cond, x)
            high_y = y_flux(t_now, k_now, t_next, k_next)
            change_z = z_change(x, t, t_now, k_now)
            for j, z in enumerate(spans):
                now, here = t_now[j], k_now[j]
                high_x = (here + cond[x + 1, rows, z]) * (field[x + 1, rows, z] - now)
                low_x = (here + cond[x - 1, rows, z]) * (now - field[x - 1, rows, z])
                new = now + (high_x - low_x) + (high_y[j] - low_y[j]) + change_z[j]
                if t:
                    new = jnp.where(keep_above if t <= ROWS else keep_below, new, 0.0)
                stores.add(put(*target(x, t, z), new))
            low_y, t_now, k_now = high_y, t_next, k_next
        stores.finish()


def thin_planes(cond, ny, store):
    tall, _, wide, _ = cond.shape
    lane = lax.broadcasted_iota(jnp.int32, (wide, LANES), 1)
    y_lane = lax.broadcasted_iota(jnp.int32, (8, LANES), 1)
    for base in range(0, tall, 16):
        planes = min(16, tall - base)
        gathered = jnp.zeros((wide, LANES), jnp.float32)
        for g in range(planes):
            piece = cond[base + g, 0]
            if g:
                piece = pltpu.roll(piece, 8 * g, 1)
            gathered = jnp.where((lane >> 3) == g, piece, gathered)
        turned = jnp.concatenate(
            [gathered, jnp.zeros((LANES - wide, LANES), jnp.float32)], axis=0
        ).T
        for g in range(planes):
            rows = turned[8 * g : 8 * g + 8, :]
            moved = pltpu.roll(rows, LANES - wide, 1)
            store(
                base + g,
                jnp.where(
                    y_lane < ny + ROWS, rows, jnp.where(y_lane >= LANES - ROWS, moved, 0.0)
                ),
            )


def mirror_rows(raw_k, ny):
    _, _, has_below, has_above = neighbours()
    upper = lax.broadcasted_iota(jnp.int32, (8, LANES), 0) < ROWS

    @pl.when(jnp.logical_not(has_above & has_below))
    def _():
        missing = (upper & jnp.logical_not(has_above)) | (
            jnp.logical_not(upper) & jnp.logical_not(has_below)
        )

        @pl.loop(0, raw_k.shape[0])
        def _(x):
            for j in range(raw_k.shape[1]):
                edge = raw_k[x, j, ny:]
                last = jnp.broadcast_to(raw_k[x, j, ny - 1 : ny, :], edge.shape)
                first = jnp.broadcast_to(raw_k[x, j, 0:1, :], edge.shape)
                raw_k[x, j, ny:] = jnp.where(missing, jnp.where(upper, last, first), edge)


def lay_out_k(loaded, place, faces, gz):
    planes, count, wide, _ = loaded.shape[1:]
    tiles = wide // 8
    spans = lane_tiles(count * LANES)
    lane = lax.broadcasted_iota(jnp.int32, (8, LANES), 1)

    @pl.loop(0, planes)
    def _(x):
        stores = Lagging(LAG)
        to = place(x)
        for t in range(tiles):
            rows = pl.ds(t, 8, stride=tiles)
            kept = slice(8 * t, 8 * t + 8)
            here = [(0.5 * step_size) * loaded[1, x, j, rows, :] for j in range(count)]
            turned = [pltpu.roll(v, LANES - 1, 1) for v in here]
            for j, z in enumerate(spans):
                deep = turned[j + 1] if j + 1 < count else here[j]
                deep = jnp.where(lane < LANES - 1, turned[j], deep)
                stores.add(put(faces, (to, kept, z), here[j]))
                stores.add(put(gz, (to, kept, z), here[j] + deep))
        stores.finish()


def lay_out_t(loaded, place, field):
    planes, count, wide, _ = loaded.shape[1:]
    tiles = wide // 8
    spans = lane_tiles(count * LANES)

    @pl.loop(0, planes)
    def _(x):
        stores = Lagging(LAG)
        to = place(x)
        for t in range(tiles):
            rows = pl.ds(t, 8, stride=tiles)
            for j, z in enumerate(spans):
                stores.add(put(field, (to, slice(8 * t, 8 * t + 8), z), loaded[0, x, j, rows, :]))
        stores.finish()


def fetch(loaded, which, ref, source_row, at, row, rows, sems):
    planes, count = ref.shape[0], loaded.shape[2]
    return [
        pltpu.make_async_copy(
            ref.at[:, pl.ds(source_row, rows), pl.ds(j * LANES, LANES)],
            loaded.at[which, pl.ds(at, planes), j, pl.ds(row, rows)],
            sems.at[j],
        )
        for j in range(count)
    ]


def own_planes_kernel(
    t_ref, k_ref, below_ref, above_ref, field, faces, gz, thin_ref, loaded, sems
):
    nx, ny, nz = t_ref.shape
    raw_t, raw_k = loaded.at[0], loaded.at[1]
    k_copies = fetch(loaded, 1, k_ref, 0, 0, 0, ny, sems.at[1])
    t_copies = fetch(loaded, 0, t_ref, 0, 0, 0, ny, sems.at[0])
    for copy in k_copies + t_copies:
        copy.start()
    upper = lax.broadcasted_iota(jnp.int32, (8, LANES), 0) < ROWS

    @pl.loop(0, nx)
    def _(x):
        for j, z in enumerate(lane_tiles(nz)):
            down, up = above_ref[x, :, z], below_ref[x, :, z]
            raw_t[x, j, ny:] = jnp.where(upper, down, pltpu.roll(up, ROWS, 0))
            raw_k[x, j, ny:] = jnp.where(upper, pltpu.roll(down, ROWS, 0), up)

    for copy in k_copies:
        copy.wait()
    thin_planes(raw_k, ny, lambda x, v: thin_ref.__setitem__(x, v))
    mirror_rows(raw_k, ny)
    lay_out_k(loaded, lambda x: x, faces, gz)
    for copy in t_copies:
        copy.wait()
    lay_out_t(loaded, lambda x: x, field)


def own_planes(temp, cond, below, above):
    nx, ny, nz = temp.shape
    wide = ny + 2 * ROWS
    hbm = pl.BlockSpec(memory_space=pl.ANY)
    vmem = pl.BlockSpec(memory_space=pltpu.VMEM)
    shape = jax.ShapeDtypeStruct((nx, wide, nz), jnp.float32)
    return pl.pallas_call(
        own_planes_kernel,
        out_shape=(shape, shape, shape, jax.ShapeDtypeStruct((nx, 8, LANES), jnp.float32)),
        in_specs=[hbm, hbm, vmem, vmem],
        scratch_shapes=[
            pltpu.VMEM((2, nx, nz // LANES, wide, LANES), jnp.float32),
            pltpu.SemaphoreType.DMA((2, nz // LANES)),
        ],
        compiler_params=params(64),
        cost_estimate=cost(nx * wide * nz * 10, 6 * nx * wide * nz * 4),
        name="own_planes",
    )(temp, cond, below, above)


def heat_kernel(
    own_field, own_faces, own_gz, own_thin, k_low, k_high, t_low, t_high, out_ref, thin_ref,
    loaded, field, between, faces, gz, placed, sems, own_sems,
):
    nx, wide, nz = own_field.shape
    ny = wide - 2 * ROWS
    tall = nx + 2 * HALO
    tiles = wide // 8
    spans = lane_tiles(nz)
    k_copies, t_copies = [], []
    for k, (k_side, t_side) in enumerate(((k_low, t_low), (k_high, t_high))):
        at = k * HALO
        k_copies += fetch(loaded, 1, k_side, 0, at, 0, ny, sems.at[3 * k])
        k_copies += fetch(loaded, 1, t_side, ny + 8, at, ny, 8, sems.at[3 * k + 1])
        t_copies += fetch(loaded, 0, t_side, 0, at, 0, ny + 8, sems.at[3 * k + 2])
    own = [
        pltpu.make_async_copy(ref, whole.at[pl.ds(HALO, nx)], own_sems.at[k])
        for k, (ref, whole) in enumerate(
            ((own_faces, faces), (own_gz, gz), (own_field, field))
        )
    ]
    for copy in k_copies + t_copies + own:
        copy.start()
    has_low, has_high, _, _ = neighbours()

    def place(x):
        return jnp.where(x < HALO, x, x + nx)

    def store_thin(x, value):
        thin_ref[x if x < HALO else x + nx] = value

    thin_ref[HALO : HALO + nx] = own_thin[...]
    raw_k = loaded.at[1]
    for copy in k_copies:
        copy.wait()
    thin_planes(raw_k, ny, store_thin)
    mirror_rows(raw_k, ny)
    lay_out_k(loaded, place, faces, gz)
    for copy in t_copies:
        copy.wait()
    lay_out_t(loaded, place, field)
    for copy in own:
        copy.wait()

    @pl.when(jnp.logical_not(has_low))
    def _():
        faces[HALO - 1] = faces[HALO]

    @pl.when(jnp.logical_not(has_high))
    def _():
        faces[HALO + nx] = faces[HALO + nx - 1]

    def inside(target):
        return lambda x, t, z: (target, (x, slice(8 * t, 8 * t + 8), z))

    def outside(x, t, z):
        return placed, (x - HALO, z.start // LANES, pl.ds(t, 8, stride=tiles))

    old, new = field, between
    for step in range(1, STEPS):
        one_step(old, faces, gz, step, tall - step, inside(new))
        for x, there in ((HALO - 1, has_low), (HALO + nx, has_high)):

            @pl.when(jnp.logical_not(there))
            def _():
                new[x] = jnp.zeros((wide, nz), jnp.float32)

        old, new = new, old
    one_step(old, faces, gz, HALO, tall - HALO, outside)

    @pl.loop(0, nx)
    def _(x):
        for j, z in enumerate(spans):
            out_ref[x, :, z] = placed[x, j, :ny, :]


def heat(own, k_low, k_high, t_low, t_high, shape):
    nx, ny, nz = shape
    tall, wide = nx + 2 * HALO, ny + 2 * ROWS
    hbm = pl.BlockSpec(memory_space=pl.ANY)
    vmem = pl.BlockSpec(memory_space=pltpu.VMEM)
    big = pltpu.VMEM((tall, wide, nz), jnp.float32)
    return pl.pallas_call(
        heat_kernel,
        out_shape=(
            jax.ShapeDtypeStruct(shape, jnp.float32),
            jax.ShapeDtypeStruct((tall, 8, LANES), jnp.float32),
        ),
        in_specs=[hbm] * 3 + [vmem] + [hbm] * 4,
        scratch_shapes=[
            pltpu.VMEM((2, 2 * HALO, nz // LANES, wide, LANES), jnp.float32),
            big,
            big,
            big,
            big,
            pltpu.VMEM((nx, nz // LANES, wide, LANES), jnp.float32),
            pltpu.SemaphoreType.DMA((6, nz // LANES)),
            pltpu.SemaphoreType.DMA((3,)),
        ],
        compiler_params=params(64),
        cost_estimate=cost(tall * wide * nz * 100, 12 * nx * ny * nz * 4),
        name="heat",
    )(*own, k_low, k_high, t_low, t_high)


def source_kernel(ny, all_ref, thin_ref, base_ref, out_ref):
    tall = thin_ref.shape[0]
    nx = tall - 2 * HALO
    sheets = all_ref.shape[1]
    sub = lax.broadcasted_iota(jnp.int32, (8, LANES), 0)
    y_lane = lax.broadcasted_iota(jnp.int32, (8, LANES), 1)

    slabs, pairs = lax.axis_size("slab"), lax.axis_size("pair")

    def sheet(down, across):
        slab = lax.axis_index("slab") + down
        pair = lax.axis_index("pair") + across
        inside = (slab >= 0) & (slab < slabs) & (pair >= 0) & (pair < pairs)
        found = all_ref[jnp.where(inside, slab * pairs + pair, 0)]
        return jnp.where(inside, found, 0.0)

    def rows_of(down):
        low, own, high = (sheet(down, across) for across in (-1, 0, 1))
        out = []
        for half in range(2):
            if half == 0:
                own_at, high_at, low_at = own, pltpu.roll(high, ny, 1), pltpu.roll(low, ny, 1)
            else:
                own_at, high_at, low_at = pltpu.roll(own, ny, 1), high, low
            out.append(
                jnp.where(
                    y_lane < ny,
                    own_at,
                    jnp.where(
                        y_lane < ny + HALO,
                        high_at,
                        jnp.where(y_lane >= LANES - HALO, low_at, 0.0),
                    ),
                )
            )
        return out

    lines = [rows_of(down) for down in (-1, 0, 1)]
    source = []
    for x in range(-HALO, nx + HALO):
        which, local = (x + nx) // nx, x % nx
        row = lines[which][local % 2][local // 2 : local // 2 + 1, :]
        source.append(jnp.where(sub == 0, jnp.broadcast_to(row, (8, LANES)), 0.0))

    cond = [thin_ref[x] for x in range(tall)]
    cx, cy, cz, centre = [], [], [], []
    for x in range(tall):
        here = cond[x]
        after = cond[min(x + 1, tall - 1)]
        before = cond[max(x - 1, 0)]
        y_after = pltpu.roll(here, LANES - 1, 1)
        y_before = pltpu.roll(here, 1, 1)
        z_after = jnp.where(sub == 7, 0.0, pltpu.roll(here, 7, 0))
        z_before = jnp.where(sub == 0, 0.0, pltpu.roll(here, 1, 0))
        cx.append(coupling(here, after))
        cy.append(coupling(here, y_after))
        cz.append(coupling(here, z_after))
        total = 6.0 * here
        for near in (after, before, y_after, y_before, z_after, z_before):
            total = total + jnp.where(near > 0.0, near, here)
        centre.append(1.0 - (0.5 * step_size) * total)

    added = source
    for step in range(1, STEPS):
        new = list(added)
        for x in range(step, tall - step):
            here = added[x]
            total = source[x] + centre[x] * here
            total = total + (cx[x] * added[x + 1] + cx[x - 1] * added[x - 1])
            total = total + cy[x] * pltpu.roll(here, LANES - 1, 1)
            total = total + pltpu.roll(cy[x] * here, 1, 1)
            total = total + cz[x] * pltpu.roll(here, 7, 0)
            new[x] = total + pltpu.roll(cz[x] * here, 1, 0)
        added = new

    lane = lax.broadcasted_iota(jnp.int32, (ny, LANES), 1)
    turned = jnp.concatenate(added[HALO : HALO + nx], axis=0).T[:ny]
    for x in range(nx):
        piece = turned if x == 0 else pltpu.roll(turned, LANES - 8 * x, 1)
        out_ref[x] = base_ref[x] + jnp.where(lane < STEPS, piece, 0.0)


def add_source(everything, thin, base):
    nx, ny, nz = base.shape
    block = pl.BlockSpec((nx, ny, LANES), lambda i: (0, 0, 0))
    return pl.pallas_call(
        functools.partial(source_kernel, ny),
        grid=(1,),
        out_shape=jax.ShapeDtypeStruct(base.shape, jnp.float32),
        in_specs=[
            pl.BlockSpec(everything.shape, lambda i: (0, 0, 0)),
            pl.BlockSpec(thin.shape, lambda i: (0, 0, 0)),
            block,
        ],
        out_specs=block,
        input_output_aliases={2: 0},
        compiler_params=params(64),
        cost_estimate=cost(1_000_000, 2 * nx * ny * LANES * 4),
        name="add_source",
    )(everything, thin, base)


def exchange(rows):
    return lax.all_to_all(rows, ("slab", "pair"), split_axis=0, concat_axis=0, tiled=True)


def together(*arrays):
    return lax.optimization_barrier(arrays)


def both_ways(low, high, axis):
    count = lax.axis_size(axis)
    forward = [(i, i + 1) for i in range(count - 1)]
    backward = [(target, source) for source, target in forward]
    from_low = lax.ppermute(high, axis, forward)
    from_high = lax.ppermute(low, axis, backward)
    return from_low, from_high


def shards(
    initial_warmth,
    heat_passing_coefficient,
    mirror_fraction,
    element_facing_site,
    tile_block_couples,
    active_slot_count,
    view_factor_blocks,
):
    nx, ny, _ = initial_warmth.shape
    slabs, pairs = lax.axis_size("slab"), lax.axis_size("pair")
    count = slabs * pairs
    blocks = mirror_fraction.shape[0]
    couples = tile_block_couples.T

    temp, cond = initial_warmth, heat_passing_coefficient
    emitted, copies = emit(temp, element_facing_site, mirror_fraction, count)
    temp, copies = together(temp, copies)

    def sweep_terms(whole):
        whole = whole.reshape(count * blocks, BLK)
        term = tile_terms(whole, couples, active_slot_count, view_factor_blocks)
        return term.reshape(count, blocks, BLK)

    whole = exchange(copies)
    cond, copies = together(cond, copies)
    send_low, send_high = cond[:HALO], cond[nx - HALO :]
    k_low, k_high = both_ways(send_low, send_high, "slab")
    whole = together(whole, send_low, send_high)[0]
    temp, cond, term = together(temp, cond, sweep_terms(whole))
    parts = exchange(term)
    below, above = both_ways(*pack_y(temp, cond), "pair")
    parts, below, above, k_low, k_high = together(parts, below, above, k_low, k_high)
    copies, below, above = together(middle(parts, emitted, mirror_fraction), below, above)
    whole = exchange(copies)
    send_low, send_high = pack_x(temp, below, above)
    t_low, t_high = both_ways(send_low, send_high, "slab")
    whole = together(whole, send_low, send_high)[0]
    temp, cond, term = together(temp, cond, sweep_terms(whole))
    parts = exchange(term)
    own = own_planes(temp, cond, below, above)
    parts, t_low, t_high, own = together(parts, t_low, t_high, own)
    radiosity, source = last(parts, emitted, mirror_fraction, element_facing_site, nx * ny, count)
    everything = exchange(source)
    own, source = together(own, source)
    base, thin = heat(own, k_low, k_high, t_low, t_high, temp.shape)

    warmed_liner = add_source(everything, thin, base)
    return (radiosity, warmed_liner)


def solution(mesh):
    return jax.shard_map(
        shards,
        mesh=mesh,
        in_specs=(
            P("slab", "pair", None),
            P("slab", "pair", None),
            P(("slab", "pair"), None),
            P(("slab", "pair"), None),
            P(("slab", "pair"), None),
            P(("slab", "pair")),
            P(("slab", "pair"), None, None),
        ),
        out_specs=(P(("slab", "pair"), None), P("slab", "pair", None)),
        check_vma=False,
    )
```

profile of v0, /device:TPU:0, one launch (start us, length us, event | category | flops | bytes accessed | tf_op | source)
XLA Modules:
  0.0 122.9 jit_solution(14420989180076966886)
XLA Ops:
  0.6 2.1 %emit.1 = (f32[16,128]{1,0:T(8,128)}, f32[32,16,128]{2,1,0:T(8,128)}) custom-call(f32[16,64,512]{2,1,0:T(8,128)} %t_ref, s32[16,128]{1,0:T(8,128)} %site_ref.3, f32[16,128]{1,0:T(8,128)} %mirror_ref.5), custom_call_target="tpu_custom_call" | custom-call | flops 10000 | bytes 900000 | tf_op jit(solution)/shard_map/emit/pallas_call | solution.py:96
  2.8 7.4 %all-to-all-start = ((f32[32,16,128]{2,1,0:T(8,128)}), f32[32,16,128]{2,1,0:T(8,128)}, u32[]{:S(2)}, u32[]{:S(2)}) async-start(f32[32,16,128]{2,1,0:T(8,128)} %get-tuple-element.48), calls=%async_computation | async-start | bytes 524288 | tf_op jit(solution)/shard_map/all_to_all | solution.py:779
  10.2 2.3 %fusion = (f32[4,64,512]{2,1,0:T(8,128)}, f32[4,64,512]{2,1,0:T(8,128)}) fusion(f32[16,64,512]{2,1,0:T(8,128)} %k_ref), kind=kLoop, calls=%fused_computation | loop fusion | bytes 2097152 | tf_op jit(solution)/shard_map/slice | solution.py:821
  12.5 4.4 %collective-permute-start.2 = (f32[4,64,512]{2,1,0:T(8,128)}, f32[4,64,512]{2,1,0:T(8,128)}, u32[]{:S(2)}, u32[]{:S(2)}) collective-permute-start(f32[4,64,512]{2,1,0:T(8,128)} %get-tuple-element.90), channel_id=1, source_target_pairs={{0,4},{4,8},{8,12},{12,16},{16,20},{20,24},{24,28},{1,5},{5,9},{9,... | collective-permute-start | bytes 1572872 | tf_op jit(solution)/shard_map/ppermute | solution.py:790
  16.8 1.3 %collective-permute-start.3 = (f32[4,64,512]{2,1,0:T(8,128)}, f32[4,64,512]{2,1,0:T(8,128)}, u32[]{:S(2)}, u32[]{:S(2)}) collective-permute-start(f32[4,64,512]{2,1,0:T(8,128)} %get-tuple-element.91), channel_id=1, source_target_pairs={{4,0},{8,4},{12,8},{16,12},{20,16},{24,20},{28,24},{5,1},{9,5},{13... | collective-permute-start | bytes 1572872 | tf_op jit(solution)/shard_map/ppermute | solution.py:791
  18.8 2.0 %all-to-all-done = f32[32,16,128]{2,1,0:T(8,128)} async-done(((f32[32,16,128]{2,1,0:T(8,128)}), f32[32,16,128]{2,1,0:T(8,128)}, u32[]{:S(2)}, u32[]{:S(2)}) %all-to-all-start) | async-done | bytes 262176 | tf_op jit(solution)/shard_map/all_to_all | solution.py:779
  20.8 7.7 %tiles.2 = f32[512,128]{1,0:T(8,128)} custom-call(s32[1]{0:T(128)S(6)} %copy.11.live_ref, s32[2,256]{1,0:T(2,128)} %bitcast.7, s32[2,256]{1,0:T(2,128)} %bitcast.8, f32[512,128]{1,0:T(8,128)} %bitcast.1.whole_ref, f32[256,128,128]{2,1,0:T(8,128)} %tiles_ref.3), custom_call_target="tpu_custom_call" | custom-call | flops 134217728 | bytes 16777216 | tf_op jit(solution)/shard_map/tiles/pallas_call | solution.py:200
  28.5 5.3 %all-to-all-start.1 = ((f32[32,16,128]{2,1,0:T(8,128)}), f32[32,16,128]{2,1,0:T(8,128)}, u32[]{:S(2)}, u32[]{:S(2)}) async-start(f32[32,16,128]{2,1,0:T(8,128)} %bitcast.5), calls=%async_computation.1 | async-start | bytes 524288 | tf_op jit(solution)/shard_map/all_to_all | solution.py:779
  33.8 2.0 %pack_y.1 = (f32[16,8,512]{2,1,0:T(8,128)}, f32[16,8,512]{2,1,0:T(8,128)}) custom-call(f32[16,64,512]{2,1,0:T(8,128)} %t_ref, f32[16,64,512]{2,1,0:T(8,128)} %k_ref, f32[16,64,512]{2,1,0:T(8,128)} %t_ref, f32[16,64,512]{2,1,0:T(8,128)} %k_ref), custom_call_target="tpu_custom_call" | custom-call | bytes 1048576 | tf_op jit(solution)/shard_map/pack_y/pallas_call | solution.py:297
  35.8 2.8 %collective-permute-start = (f32[16,8,512]{2,1,0:T(8,128)}, f32[16,8,512]{2,1,0:T(8,128)}, u32[]{:S(2)}, u32[]{:S(2)}) collective-permute-start(f32[16,8,512]{2,1,0:T(8,128)} %get-tuple-element.54), channel_id=1, source_target_pairs={{0,1},{1,2},{2,3},{4,5},{5,6},{6,7},{8,9},{9,10},{10,11},{12,13},{... | collective-permute-start | bytes 786440 | tf_op jit(solution)/shard_map/ppermute | solution.py:790
  38.6 1.3 %collective-permute-start.1 = (f32[16,8,512]{2,1,0:T(8,128)}, f32[16,8,512]{2,1,0:T(8,128)}, u32[]{:S(2)}, u32[]{:S(2)}) collective-permute-start(f32[16,8,512]{2,1,0:T(8,128)} %get-tuple-element.55), channel_id=1, source_target_pairs={{1,0},{2,1},{3,2},{5,4},{6,5},{7,6},{9,8},{10,9},{11,10},{13,12},{... | collective-permute-start | bytes 786440 | tf_op jit(solution)/shard_map/ppermute | solution.py:791
  39.9 2.2 %collective-permute-done.2.k_low = f32[4,64,512]{2,1,0:T(8,128)} collective-permute-done((f32[4,64,512]{2,1,0:T(8,128)}, f32[4,64,512]{2,1,0:T(8,128)}, u32[]{:S(2)}, u32[]{:S(2)}) %collective-permute-start.2) | collective-permute-done | bytes 524320 | tf_op jit(solution)/shard_map/ppermute | solution.py:790
  42.1 0.0 collective-permute-done.3.k_high
  42.1 0.0 collective-permute-done.below0.below1.below_ref
  42.1 0.7 collective-permute-done.1.above0.above1.above_ref
  42.8 1.5 %all-to-all-done.1.parts_ref = f32[32,16,128]{2,1,0:T(8,128)} async-done(((f32[32,16,128]{2,1,0:T(8,128)}), f32[32,16,128]{2,1,0:T(8,128)}, u32[]{:S(2)}, u32[]{:S(2)}) %all-to-all-start.1) | async-done | bytes 262176 | tf_op jit(solution)/shard_map/all_to_all | solution.py:779
  44.3 1.7 %middle.1 = f32[32,16,128]{2,1,0:T(8,128)} custom-call(f32[32,16,128]{2,1,0:T(8,128)} %all-to-all-done.1.parts_ref, f32[16,128]{1,0:T(8,128)} %get-tuple-element.57.emitted_ref, f32[16,128]{1,0:T(8,128)} %mirror_ref.5), custom_call_target="tpu_custom_call" | custom-call | flops 100000 | bytes 600000 | tf_op jit(solution)/shard_map/middle/pallas_call | solution.py:233
  46.1 7.6 %all-to-all-start.2 = ((f32[32,16,128]{2,1,0:T(8,128)}), f32[32,16,128]{2,1,0:T(8,128)}, u32[]{:S(2)}, u32[]{:S(2)}) async-start(f32[32,16,128]{2,1,0:T(8,128)} %middle.1), calls=%async_computation.2 | async-start | bytes 524288 | tf_op jit(solution)/shard_map/all_to_all | solution.py:779
  53.6 2.4 %pack_x.1 = (f32[4,80,512]{2,1,0:T(8,128)}, f32[4,80,512]{2,1,0:T(8,128)}) custom-call(f32[16,64,512]{2,1,0:T(8,128)} %t_ref, f32[16,64,512]{2,1,0:T(8,128)} %t_ref, f32[16,8,512]{2,1,0:T(8,128)} %collective-permute-done.below0.below1.below_ref, f32[16,8,512]{2,1,0:T(8,128)} %collective-permute-done.1.above0.above1.above_ref, ...), custom_call_target="tpu_custom_call" | custom-call | bytes 2621440 | tf_op jit(solution)/shard_map/pack_x/pallas_call | solution.py:335
  56.1 1.3 %collective-permute-start.5 = (f32[4,80,512]{2,1,0:T(8,128)}, f32[4,80,512]{2,1,0:T(8,128)}, u32[]{:S(2)}, u32[]{:S(2)}) collective-permute-start(f32[4,80,512]{2,1,0:T(8,128)} %get-tuple-element.63), channel_id=1, source_target_pairs={{4,0},{8,4},{12,8},{16,12},{20,16},{24,20},{28,24},{5,1},{9,5},{13... | collective-permute-start | bytes 1966088 | tf_op jit(solution)/shard_map/ppermute | solution.py:791
  57.3 5.4 %collective-permute-start.4 = (f32[4,80,512]{2,1,0:T(8,128)}, f32[4,80,512]{2,1,0:T(8,128)}, u32[]{:S(2)}, u32[]{:S(2)}) collective-permute-start(f32[4,80,512]{2,1,0:T(8,128)} %get-tuple-element.64), channel_id=1, source_target_pairs={{0,4},{4,8},{8,12},{12,16},{16,20},{20,24},{24,28},{1,5},{5,9},{9,... | collective-permute-start | bytes 1966088 | tf_op jit(solution)/shard_map/ppermute | solution.py:790
  62.7 1.5 %all-to-all-done.2 = f32[32,16,128]{2,1,0:T(8,128)} async-done(((f32[32,16,128]{2,1,0:T(8,128)}), f32[32,16,128]{2,1,0:T(8,128)}, u32[]{:S(2)}, u32[]{:S(2)}) %all-to-all-start.2) | async-done | bytes 262176 | tf_op jit(solution)/shard_map/all_to_all | solution.py:779
  64.2 7.7 %tiles.3 = f32[512,128]{1,0:T(8,128)} custom-call(s32[1]{0:T(128)S(6)} %copy.11.live_ref, s32[2,256]{1,0:T(2,128)} %bitcast.9, s32[2,256]{1,0:T(2,128)} %bitcast.10, f32[512,128]{1,0:T(8,128)} %bitcast.3.whole_ref, f32[256,128,128]{2,1,0:T(8,128)} %tiles_ref.3), custom_call_target="tpu_custom_call" | custom-call | flops 134217728 | bytes 16777216 | tf_op jit(solution)/shard_map/tiles/pallas_call | solution.py:200
  71.9 5.4 %all-to-all-start.3 = ((f32[32,16,128]{2,1,0:T(8,128)}), f32[32,16,128]{2,1,0:T(8,128)}, u32[]{:S(2)}, u32[]{:S(2)}) async-start(f32[32,16,128]{2,1,0:T(8,128)} %bitcast.6), calls=%async_computation.3 | async-start | bytes 524288 | tf_op jit(solution)/shard_map/all_to_all | solution.py:779
  77.3 7.9 %own_planes.1 = (f32[16,72,512]{2,1,0:T(8,128)}, f32[16,72,512]{2,1,0:T(8,128)}, f32[16,72,512]{2,1,0:T(8,128)}, f32[16,8,128]{2,1,0:T(8,128)}) custom-call(f32[16,64,512]{2,1,0:T(8,128)} %t_ref, f32[16,64,512]{2,1,0:T(8,128)} %k_ref, f32[16,8,512]{2,1,0:T(8,128)} %collective-permute-done.below0.below1.below_ref, ...), custom_call_target="tpu_custom_call" | custom-call | flops 5898240 | bytes 14155776 | tf_op jit(solution)/shard_map/own_planes/pallas_call | solution.py:557
  85.3 0.0 collective-permute-done.5.t_high
  85.3 7.1 %collective-permute-done.4.t_low = f32[4,80,512]{2,1,0:T(8,128)} collective-permute-done((f32[4,80,512]{2,1,0:T(8,128)}, f32[4,80,512]{2,1,0:T(8,128)}, u32[]{:S(2)}, u32[]{:S(2)}) %collective-permute-start.4) | collective-permute-done | bytes 655392 | tf_op jit(solution)/shard_map/ppermute | solution.py:790
  92.3 0.2 all-to-all-done.3.parts_ref
  92.5 2.2 %last.1 = (f32[16,128]{1,0:T(8,128)}, f32[32,8,128]{2,1,0:T(8,128)}) custom-call(f32[32,16,128]{2,1,0:T(8,128)} %all-to-all-done.3.parts_ref, f32[16,128]{1,0:T(8,128)} %get-tuple-element.57.emitted_ref, f32[16,128]{1,0:T(8,128)} %mirror_ref.5, s32[16,128]{1,0:T(8,128)} %site_ref.3), custom_call_target="tpu_custom_call" | custom-call | flops 10000000 | bytes 600000 | tf_op jit(solution)/shard_map/last/pallas_call | solution.py:273
  94.7 5.1 %all-to-all-start.4 = ((f32[32,8,128]{2,1,0:T(8,128)}), f32[32,8,128]{2,1,0:T(8,128)}, u32[]{:S(2)}, u32[]{:S(2)}) async-start(f32[32,8,128]{2,1,0:T(8,128)} %get-tuple-element.75), calls=%async_computation.4 | async-start | bytes 262144 | tf_op jit(solution)/shard_map/all_to_all | solution.py:779
  99.8 20.5 %heat.1 = (f32[16,64,512]{2,1,0:T(8,128)}, f32[24,8,128]{2,1,0:T(8,128)}) custom-call(f32[16,72,512]{2,1,0:T(8,128)} %get-tuple-element.80.own_field, f32[16,72,512]{2,1,0:T(8,128)} %get-tuple-element.81.own_faces, f32[16,72,512]{2,1,0:T(8,128)} %get-tuple-element.82.own_gz, f32[16,8,128]{2,1,0:T(8,128)} %get-tuple-element.83.own_thin, ...), custom_call_target="tpu_custom_call" | custom-call | flops 88473600 | bytes 25165824 | tf_op jit(solution)/shard_map/heat/pallas_call | solution.py:653
  120.3 0.0 all-to-all-done.4.all_ref
  120.3 2.6 %add_source.1 = f32[16,64,512]{2,1,0:T(8,128)} custom-call(f32[32,8,128]{2,1,0:T(8,128)} %all-to-all-done.4.all_ref, f32[24,8,128]{2,1,0:T(8,128)} %get-tuple-element.88.thin_ref, f32[16,64,512]{2,1,0:T(8,128)} %get-tuple-element.89.base_ref), custom_call_target="tpu_custom_call", output_to_operand_aliasing={{}: (2, {})} | custom-call | flops 1000000 | bytes 1048576 | tf_op jit(solution)/shard_map/add_source/pallas_call | solution.py:761
Async XLA Ops:
  2.8 18.0 %all-to-all-start = ((f32[32,16,128]{2,1,0:T(8,128)}), f32[32,16,128]{2,1,0:T(8,128)}, u32[]{:S(2)}, u32[]{:S(2)}) async-start(f32[32,16,128]{2,1,0:T(8,128)} %get-tuple-element.48), calls=%async_computation | async-start | bytes 524288 | tf_op jit(solution)/shard_map/all_to_all | solution.py:779
  12.5 29.6 %collective-permute-start.2 = (f32[4,64,512]{2,1,0:T(8,128)}, f32[4,64,512]{2,1,0:T(8,128)}, u32[]{:S(2)}, u32[]{:S(2)}) collective-permute-start(f32[4,64,512]{2,1,0:T(8,128)} %get-tuple-element.90), channel_id=1, source_target_pairs={{0,4},{4,8},{8,12},{12,16},{16,20},{20,24},{24,28},{1,5},{5,9},{9,... | collective-permute-start | bytes 1572872 | tf_op jit(solution)/shard_map/ppermute | solution.py:790
  16.8 25.2 %collective-permute-start.3 = (f32[4,64,512]{2,1,0:T(8,128)}, f32[4,64,512]{2,1,0:T(8,128)}, u32[]{:S(2)}, u32[]{:S(2)}) collective-permute-start(f32[4,64,512]{2,1,0:T(8,128)} %get-tuple-element.91), channel_id=1, source_target_pairs={{4,0},{8,4},{12,8},{16,12},{20,16},{24,20},{28,24},{5,1},{9,5},{13... | collective-permute-start | bytes 1572872 | tf_op jit(solution)/shard_map/ppermute | solution.py:791
  28.5 15.8 %all-to-all-start.1 = ((f32[32,16,128]{2,1,0:T(8,128)}), f32[32,16,128]{2,1,0:T(8,128)}, u32[]{:S(2)}, u32[]{:S(2)}) async-start(f32[32,16,128]{2,1,0:T(8,128)} %bitcast.5), calls=%async_computation.1 | async-start | bytes 524288 | tf_op jit(solution)/shard_map/all_to_all | solution.py:779
  35.8 6.3 %collective-permute-start = (f32[16,8,512]{2,1,0:T(8,128)}, f32[16,8,512]{2,1,0:T(8,128)}, u32[]{:S(2)}, u32[]{:S(2)}) collective-permute-start(f32[16,8,512]{2,1,0:T(8,128)} %get-tuple-element.54), channel_id=1, source_target_pairs={{0,1},{1,2},{2,3},{4,5},{5,6},{6,7},{8,9},{9,10},{10,11},{12,13},{... | collective-permute-start | bytes 786440 | tf_op jit(solution)/shard_map/ppermute | solution.py:790
  38.6 4.2 %collective-permute-start.1 = (f32[16,8,512]{2,1,0:T(8,128)}, f32[16,8,512]{2,1,0:T(8,128)}, u32[]{:S(2)}, u32[]{:S(2)}) collective-permute-start(f32[16,8,512]{2,1,0:T(8,128)} %get-tuple-element.55), channel_id=1, source_target_pairs={{1,0},{2,1},{3,2},{5,4},{6,5},{7,6},{9,8},{10,9},{11,10},{13,12},{... | collective-permute-start | bytes 786440 | tf_op jit(solution)/shard_map/ppermute | solution.py:791
  46.1 18.1 %all-to-all-start.2 = ((f32[32,16,128]{2,1,0:T(8,128)}), f32[32,16,128]{2,1,0:T(8,128)}, u32[]{:S(2)}, u32[]{:S(2)}) async-start(f32[32,16,128]{2,1,0:T(8,128)} %middle.1), calls=%async_computation.2 | async-start | bytes 524288 | tf_op jit(solution)/shard_map/all_to_all | solution.py:779
  56.1 29.2 %collective-permute-start.5 = (f32[4,80,512]{2,1,0:T(8,128)}, f32[4,80,512]{2,1,0:T(8,128)}, u32[]{:S(2)}, u32[]{:S(2)}) collective-permute-start(f32[4,80,512]{2,1,0:T(8,128)} %get-tuple-element.63), channel_id=1, source_target_pairs={{4,0},{8,4},{12,8},{16,12},{20,16},{24,20},{28,24},{5,1},{9,5},{13... | collective-permute-start | bytes 1966088 | tf_op jit(solution)/shard_map/ppermute | solution.py:791
  57.3 35.0 %collective-permute-start.4 = (f32[4,80,512]{2,1,0:T(8,128)}, f32[4,80,512]{2,1,0:T(8,128)}, u32[]{:S(2)}, u32[]{:S(2)}) collective-permute-start(f32[4,80,512]{2,1,0:T(8,128)} %get-tuple-element.64), channel_id=1, source_target_pairs={{0,4},{4,8},{8,12},{12,16},{16,20},{20,24},{24,28},{1,5},{5,9},{9,... | collective-permute-start | bytes 1966088 | tf_op jit(solution)/shard_map/ppermute | solution.py:790
  71.9 20.6 %all-to-all-start.3 = ((f32[32,16,128]{2,1,0:T(8,128)}), f32[32,16,128]{2,1,0:T(8,128)}, u32[]{:S(2)}, u32[]{:S(2)}) async-start(f32[32,16,128]{2,1,0:T(8,128)} %bitcast.6), calls=%async_computation.3 | async-start | bytes 524288 | tf_op jit(solution)/shard_map/all_to_all | solution.py:779
  94.7 25.6 %all-to-all-start.4 = ((f32[32,8,128]{2,1,0:T(8,128)}), f32[32,8,128]{2,1,0:T(8,128)}, u32[]{:S(2)}, u32[]{:S(2)}) async-start(f32[32,8,128]{2,1,0:T(8,128)} %get-tuple-element.75), calls=%async_computation.4 | async-start | bytes 262144 | tf_op jit(solution)/shard_map/all_to_all | solution.py:779
where the time goes:
time: 124 us; the launch traced here: 123 us
  Pallas kernels  57 us (46%)
  starting transfers between devices  47.2 us (38%)
  waiting for transfers between devices  15.1 us (12%)
  local copies, waits for them, and re-layouts  2.25 us (2%)
  between operations  1.4 us (1%)
    all_to_all x5, starting transfers between devices, exchange(): lax.all_to_all(rows, ('slab', 'pair'), split_axis=0, concat_axis=0, tiled...  30.7 us
    pallas_call x1, Pallas kernels, heat(): pl.pallas_call(heat_kernel, out_shape=(jax.ShapeDtypeStruct(shape, jnp.fl...  20.5 us
    pallas_call x2, Pallas kernels, tile_terms(): pl.pallas_call(tiles_kernel, out_shape=jax.ShapeDtypeStruct(whole.shape,...  15.4 us
    ppermute x3, starting transfers between devices, both_ways(): from_low = lax.ppermute(high, axis, forward)  12.6 us
    ppermute x3, waiting for transfers between devices, both_ways(): from_low = lax.ppermute(high, axis, forward)  9.24 us
    pallas_call x1, Pallas kernels, own_planes(): pl.pallas_call(own_planes_kernel, out_shape=(shape, shape, shape, jax.Sha...  7.95 us
    all_to_all x5, waiting for transfers between devices, exchange(): lax.all_to_all(rows, ('slab', 'pair'), split_axis=0, concat_axis=0, tiled...  5.15 us
    ppermute x3, starting transfers between devices, both_ways(): from_high = lax.ppermute(low, axis, backward)  3.84 us
  transfers between devices with their start and end apart: 11, of which 7 were waited for; matrix products, arithmetic and copies ran while one was open for 2% of the time, Pallas kernels for 39%

commit v1 on v0

--- a/solution.py
+++ b/solution.py
@@ -306,17 +306,38 @@
     )(temp, cond, temp, cond)
 
 
+def mixed_tile(t_tile, k_tile):
+    row = lax.broadcasted_iota(jnp.int32, t_tile.shape, 0)
+    of_k = jnp.where(row < 4, pltpu.roll(k_tile, 2, 0), pltpu.roll(k_tile, 6, 0))
+    return jnp.where((row < 2) | (row >= 6), t_tile, of_k)
+
+
+def unmixed(tile):
+    row = lax.broadcasted_iota(jnp.int32, tile.shape, 0)
+    outer = (row < 2) | (row >= 6)
+    of_k = jnp.where(row < 4, pltpu.roll(tile, 6, 0), pltpu.roll(tile, 2, 0))
+    return jnp.where(outer, tile, 0.0), jnp.where(outer, of_k, 0.0)
+
+
 def pack_x_kernel(first, final, below0, above0, below1, above1, low_ref, high_ref):
     ny, nz = first.shape[1:]
     upper = lax.broadcasted_iota(jnp.int32, (8, nz), 0) < ROWS
-    for send, temp, below, above in (
-        (low_ref, first, below0, above0),
-        (high_ref, final, below1, above1),
+    tail = HALO * ny
+    for send, temp, below, above, order in (
+        (low_ref, first, below0, above0, (0, 1, 2)),
+        (high_ref, final, below1, above1, (HALO - 1, HALO - 2, HALO - 3)),
     ):
         for p in range(HALO):
-            send[p, :ny] = temp[p]
-            send[p, ny : ny + 8] = jnp.where(upper, above[p], pltpu.roll(below[p], ROWS, 0))
-            send[p, ny + 8 :] = jnp.where(upper, pltpu.roll(above[p], ROWS, 0), below[p])
+            send[p * ny : (p + 1) * ny, :] = temp[p]
+        for k, p in enumerate(order):
+            t_tile = jnp.where(upper, above[p], pltpu.roll(below[p], ROWS, 0))
+            k_tile = jnp.where(upper, pltpu.roll(above[p], ROWS, 0), below[p])
+            if k == 0:
+                send[tail : tail + 8, :] = t_tile
+                send[tail + 8 : tail + 16, :] = k_tile
+            else:
+                at = tail + 8 + 8 * k
+                send[at : at + 8, :] = mixed_tile(t_tile, k_tile)
 
 
 def pack_x(temp, below, above):
@@ -330,8 +351,9 @@
 
     first, final = ends(ny)
     first_rows, final_rows = ends(8)
-    whole = pl.BlockSpec((HALO, ny + 16, nz), lambda i: (0, 0, 0))
-    shape = jax.ShapeDtypeStruct((HALO, ny + 16, nz), jnp.float32)
+    rows = HALO * ny + 32
+    whole = pl.BlockSpec((rows, nz), lambda i: (0, 0))
+    shape = jax.ShapeDtypeStruct((rows, nz), jnp.float32)
     return pl.pallas_call(
         pack_x_kernel,
         grid=(1,),
@@ -339,7 +361,7 @@
         in_specs=[first, final, first_rows, first_rows, final_rows, final_rows],
         out_specs=(whole, whole),
         compiler_params=params(64),
-        cost_estimate=cost(0, 4 * HALO * (ny + 16) * nz * 4),
+        cost_estimate=cost(0, 4 * rows * nz * 4),
         name="pack_x",
     )(temp, temp, below, above, below, above)
 
@@ -570,7 +592,7 @@
 
 def heat_kernel(
     own_field, own_faces, own_gz, own_thin, k_low, k_high, t_low, t_high, out_ref, thin_ref,
-    loaded, field, between, faces, gz, placed, sems, own_sems,
+    loaded, corners, field, between, faces, gz, placed, sems, own_sems,
 ):
     nx, wide, nz = own_field.shape
     ny = wide - 2 * ROWS
@@ -581,8 +603,20 @@
     for k, (k_side, t_side) in enumerate(((k_low, t_low), (k_high, t_high))):
         at = k * HALO
         k_copies += fetch(loaded, 1, k_side, 0, at, 0, ny, sems.at[3 * k])
-        k_copies += fetch(loaded, 1, t_side, ny + 8, at, ny, 8, sems.at[3 * k + 1])
-        t_copies += fetch(loaded, 0, t_side, 0, at, 0, ny + 8, sems.at[3 * k + 2])
+        k_copies.append(
+            pltpu.make_async_copy(
+                t_side.at[pl.ds(HALO * ny, 32)], corners.at[k], own_sems.at[3 + k]
+            )
+        )
+        for p in range(HALO):
+            t_copies += [
+                pltpu.make_async_copy(
+                    t_side.at[pl.ds(p * ny, ny), pl.ds(j * LANES, LANES)],
+                    loaded.at[0, at + p, j, pl.ds(0, ny)],
+                    sems.at[3 * (k + 1) - 1 + 6 * p, j],
+                )
+                for j in range(len(spans))
+            ]
     own = [
         pltpu.make_async_copy(ref, whole.at[pl.ds(HALO, nx)], own_sems.at[k])
         for k, (ref, whole) in enumerate(
@@ -600,9 +634,22 @@
         thin_ref[x if x < HALO else x + nx] = value
 
     thin_ref[HALO : HALO + nx] = own_thin[...]
-    raw_k = loaded.at[1]
+    raw_t, raw_k = loaded.at[0], loaded.at[1]
     for copy in k_copies:
         copy.wait()
+    for k, order in enumerate(
+        ((HALO - 1, HALO - 2, HALO - 3, 0), (HALO, HALO + 1, HALO + 2, 2 * HALO - 1))
+    ):
+        for distance, p in enumerate(order):
+            for j, z in enumerate(spans):
+                if distance == 0:
+                    t_tile, k_tile = corners[k, :8, z], corners[k, 8:16, z]
+                elif distance + 1 < HALO:
+                    t_tile, k_tile = unmixed(corners[k, 8 + 8 * distance : 16 + 8 * distance, z])
+                else:
+                    t_tile = k_tile = jnp.zeros((8, LANES), jnp.float32)
+                raw_t[p, j, ny:] = t_tile
+                raw_k[p, j, ny:] = k_tile
     thin_planes(raw_k, ny, store_thin)
     mirror_rows(raw_k, ny)
     lay_out_k(loaded, place, faces, gz)
@@ -659,13 +706,14 @@
         in_specs=[hbm] * 3 + [vmem] + [hbm] * 4,
         scratch_shapes=[
             pltpu.VMEM((2, 2 * HALO, nz // LANES, wide, LANES), jnp.float32),
+            pltpu.VMEM((2, 32, nz), jnp.float32),
             big,
             big,
             big,
             big,
             pltpu.VMEM((nx, nz // LANES, wide, LANES), jnp.float32),
-            pltpu.SemaphoreType.DMA((6, nz // LANES)),
-            pltpu.SemaphoreType.DMA((3,)),
+            pltpu.SemaphoreType.DMA((6 * HALO, nz // LANES)),
+            pltpu.SemaphoreType.DMA((5,)),
         ],
         compiler_params=params(64),
         cost_estimate=cost(tall * wide * nz * 100, 12 * nx * ny * nz * 4),

time: 124 us -> 122 us (0.984)
  waiting for transfers between devices: 15.1 us -> 11.8 us
    ppermute x3, waiting for transfers between devices: 9.24 us -> 5.16 us  [both_ways(): from_low = lax.ppermute(high, axis, forward)]
  transfers between devices with their start and end apart: 11 -> 11, of which waited for: 7 -> 7; matrix products, arithmetic and copies ran while one was open for 2% -> 2% of each run, Pallas kernels for 39% -> 40%
where the time goes in v1:
time: 122 us; the launch traced here: 121 us
  Pallas kernels  57.4 us (47%)
  starting transfers between devices  48.2 us (40%)
  waiting for transfers between devices  11.8 us (10%)
  local copies, waits for them, and re-layouts  2.25 us (2%)
  between operations  1.4 us (1%)
    all_to_all x5, starting transfers between devices, exchange(): lax.all_to_all(rows, ('slab', 'pair'), split_axis=0, concat_axis=0, tiled...  31.8 us
    pallas_call x1, Pallas kernels, heat(): pl.pallas_call(heat_kernel, out_shape=(jax.ShapeDtypeStruct(shape, jnp.fl...  21 us
    pallas_call x2, Pallas kernels, tile_terms(): pl.pallas_call(tiles_kernel, out_shape=jax.ShapeDtypeStruct(whole.shape,...  15.5 us
    ppermute x3, starting transfers between devices, both_ways(): from_low = lax.ppermute(high, axis, forward)  12.6 us
    pallas_call x1, Pallas kernels, own_planes(): pl.pallas_call(own_planes_kernel, out_shape=(shape, shape, shape, jax.Sha...  7.93 us
    all_to_all x5, waiting for transfers between devices, exchange(): lax.all_to_all(rows, ('slab', 'pair'), split_axis=0, concat_axis=0, tiled...  5.25 us
    ppermute x3, waiting for transfers between devices, both_ways(): from_low = lax.ppermute(high, axis, forward)  5.16 us
    ppermute x3, starting transfers between devices, both_ways(): from_high = lax.ppermute(low, axis, backward)  3.84 us
  transfers between devices with their start and end apart: 11, of which 7 were waited for; matrix products, arithmetic and copies ran while one was open for 2% of the time, Pallas kernels for 40%

profile of v1, /device:TPU:0, one launch (start us, length us, event | category | flops | bytes accessed | tf_op | source)
XLA Modules:
  0.0 121.0 jit_solution(7243083290541012219)
XLA Ops:
  0.6 2.1 %emit.1 = (f32[16,128]{1,0:T(8,128)}, f32[32,16,128]{2,1,0:T(8,128)}) custom-call(f32[16,64,512]{2,1,0:T(8,128)} %t_ref, s32[16,128]{1,0:T(8,128)} %site_ref.3, f32[16,128]{1,0:T(8,128)} %mirror_ref.5), custom_call_target="tpu_custom_call" | custom-call | flops 10000 | bytes 900000 | tf_op jit(solution)/shard_map/emit/pallas_call | solution.py:96
  2.8 7.4 %all-to-all-start = ((f32[32,16,128]{2,1,0:T(8,128)}), f32[32,16,128]{2,1,0:T(8,128)}, u32[]{:S(2)}, u32[]{:S(2)}) async-start(f32[32,16,128]{2,1,0:T(8,128)} %get-tuple-element.48), calls=%async_computation | async-start | bytes 524288 | tf_op jit(solution)/shard_map/all_to_all | solution.py:827
  10.2 2.3 %fusion = (f32[4,64,512]{2,1,0:T(8,128)}, f32[4,64,512]{2,1,0:T(8,128)}) fusion(f32[16,64,512]{2,1,0:T(8,128)} %k_ref), kind=kLoop, calls=%fused_computation | loop fusion | bytes 2097152 | tf_op jit(solution)/shard_map/slice | solution.py:869
  12.5 4.4 %collective-permute-start.2 = (f32[4,64,512]{2,1,0:T(8,128)}, f32[4,64,512]{2,1,0:T(8,128)}, u32[]{:S(2)}, u32[]{:S(2)}) collective-permute-start(f32[4,64,512]{2,1,0:T(8,128)} %get-tuple-element.90), channel_id=1, source_target_pairs={{0,4},{4,8},{8,12},{12,16},{16,20},{20,24},{24,28},{1,5},{5,9},{9,... | collective-permute-start | bytes 1572872 | tf_op jit(solution)/shard_map/ppermute | solution.py:838
  16.9 1.3 %collective-permute-start.3 = (f32[4,64,512]{2,1,0:T(8,128)}, f32[4,64,512]{2,1,0:T(8,128)}, u32[]{:S(2)}, u32[]{:S(2)}) collective-permute-start(f32[4,64,512]{2,1,0:T(8,128)} %get-tuple-element.91), channel_id=1, source_target_pairs={{4,0},{8,4},{12,8},{16,12},{20,16},{24,20},{28,24},{5,1},{9,5},{13... | collective-permute-start | bytes 1572872 | tf_op jit(solution)/shard_map/ppermute | solution.py:839
  18.8 2.0 %all-to-all-done = f32[32,16,128]{2,1,0:T(8,128)} async-done(((f32[32,16,128]{2,1,0:T(8,128)}), f32[32,16,128]{2,1,0:T(8,128)}, u32[]{:S(2)}, u32[]{:S(2)}) %all-to-all-start) | async-done | bytes 262176 | tf_op jit(solution)/shard_map/all_to_all | solution.py:827
  20.8 7.7 %tiles.2 = f32[512,128]{1,0:T(8,128)} custom-call(s32[1]{0:T(128)S(6)} %copy.11.live_ref, s32[2,256]{1,0:T(2,128)} %bitcast.7, s32[2,256]{1,0:T(2,128)} %bitcast.8, f32[512,128]{1,0:T(8,128)} %bitcast.1.whole_ref, f32[256,128,128]{2,1,0:T(8,128)} %tiles_ref.3), custom_call_target="tpu_custom_call" | custom-call | flops 134217728 | bytes 16777216 | tf_op jit(solution)/shard_map/tiles/pallas_call | solution.py:200
  28.5 5.7 %all-to-all-start.1 = ((f32[32,16,128]{2,1,0:T(8,128)}), f32[32,16,128]{2,1,0:T(8,128)}, u32[]{:S(2)}, u32[]{:S(2)}) async-start(f32[32,16,128]{2,1,0:T(8,128)} %bitcast.5), calls=%async_computation.1 | async-start | bytes 524288 | tf_op jit(solution)/shard_map/all_to_all | solution.py:827
  34.2 2.0 %pack_y.1 = (f32[16,8,512]{2,1,0:T(8,128)}, f32[16,8,512]{2,1,0:T(8,128)}) custom-call(f32[16,64,512]{2,1,0:T(8,128)} %t_ref, f32[16,64,512]{2,1,0:T(8,128)} %k_ref, f32[16,64,512]{2,1,0:T(8,128)} %t_ref, f32[16,64,512]{2,1,0:T(8,128)} %k_ref), custom_call_target="tpu_custom_call" | custom-call | bytes 1048576 | tf_op jit(solution)/shard_map/pack_y/pallas_call | solution.py:297
  36.3 2.8 %collective-permute-start = (f32[16,8,512]{2,1,0:T(8,128)}, f32[16,8,512]{2,1,0:T(8,128)}, u32[]{:S(2)}, u32[]{:S(2)}) collective-permute-start(f32[16,8,512]{2,1,0:T(8,128)} %get-tuple-element.54), channel_id=1, source_target_pairs={{0,1},{1,2},{2,3},{4,5},{5,6},{6,7},{8,9},{9,10},{10,11},{12,13},{... | collective-permute-start | bytes 786440 | tf_op jit(solution)/shard_map/ppermute | solution.py:838
  39.0 1.3 %collective-permute-start.1 = (f32[16,8,512]{2,1,0:T(8,128)}, f32[16,8,512]{2,1,0:T(8,128)}, u32[]{:S(2)}, u32[]{:S(2)}) collective-permute-start(f32[16,8,512]{2,1,0:T(8,128)} %get-tuple-element.55), channel_id=1, source_target_pairs={{1,0},{2,1},{3,2},{5,4},{6,5},{7,6},{9,8},{10,9},{11,10},{13,12},{... | collective-permute-start | bytes 786440 | tf_op jit(solution)/shard_map/ppermute | solution.py:839
  40.3 1.6 %collective-permute-done.2.k_low = f32[4,64,512]{2,1,0:T(8,128)} collective-permute-done((f32[4,64,512]{2,1,0:T(8,128)}, f32[4,64,512]{2,1,0:T(8,128)}, u32[]{:S(2)}, u32[]{:S(2)}) %collective-permute-start.2) | collective-permute-done | bytes 524320 | tf_op jit(solution)/shard_map/ppermute | solution.py:838
  41.9 0.0 collective-permute-done.3.k_high
  41.9 0.0 collective-permute-done.below0.below1.below_ref
  41.9 1.3 %collective-permute-done.1.above0.above1.above_ref = f32[16,8,512]{2,1,0:T(8,128)} collective-permute-done((f32[16,8,512]{2,1,0:T(8,128)}, f32[16,8,512]{2,1,0:T(8,128)}, u32[]{:S(2)}, u32[]{:S(2)}) %collective-permute-start.1) | collective-permute-done | bytes 262176 | tf_op jit(solution)/shard_map/ppermute | solution.py:839
  43.3 1.5 %all-to-all-done.1.parts_ref = f32[32,16,128]{2,1,0:T(8,128)} async-done(((f32[32,16,128]{2,1,0:T(8,128)}), f32[32,16,128]{2,1,0:T(8,128)}, u32[]{:S(2)}, u32[]{:S(2)}) %all-to-all-start.1) | async-done | bytes 262176 | tf_op jit(solution)/shard_map/all_to_all | solution.py:827
  44.8 1.7 %middle.1 = f32[32,16,128]{2,1,0:T(8,128)} custom-call(f32[32,16,128]{2,1,0:T(8,128)} %all-to-all-done.1.parts_ref, f32[16,128]{1,0:T(8,128)} %get-tuple-element.57.emitted_ref, f32[16,128]{1,0:T(8,128)} %mirror_ref.5), custom_call_target="tpu_custom_call" | custom-call | flops 100000 | bytes 600000 | tf_op jit(solution)/shard_map/middle/pallas_call | solution.py:233
  46.5 7.6 %all-to-all-start.2 = ((f32[32,16,128]{2,1,0:T(8,128)}), f32[32,16,128]{2,1,0:T(8,128)}, u32[]{:S(2)}, u32[]{:S(2)}) async-start(f32[32,16,128]{2,1,0:T(8,128)} %middle.1), calls=%async_computation.2 | async-start | bytes 524288 | tf_op jit(solution)/shard_map/all_to_all | solution.py:827
  54.1 2.3 %pack_x.1 = (f32[288,512]{1,0:T(8,128)}, f32[288,512]{1,0:T(8,128)}) custom-call(f32[16,64,512]{2,1,0:T(8,128)} %t_ref, f32[16,64,512]{2,1,0:T(8,128)} %t_ref, f32[16,8,512]{2,1,0:T(8,128)} %collective-permute-done.below0.below1.below_ref, f32[16,8,512]{2,1,0:T(8,128)} %collective-permute-done.1.above0.above1.above_ref, ...), custom_call_target="tpu_custom_call" | custom-call | bytes 2359296 | tf_op jit(solution)/shard_map/pack_x/pallas_call | solution.py:357
  56.4 1.3 %collective-permute-start.5 = (f32[288,512]{1,0:T(8,128)}, f32[288,512]{1,0:T(8,128)}, u32[]{:S(2)}, u32[]{:S(2)}) collective-permute-start(f32[288,512]{1,0:T(8,128)} %get-tuple-element.63), channel_id=1, source_target_pairs={{4,0},{8,4},{12,8},{16,12},{20,16},{24,20},{28,24},{5,1},{9,5},{13... | collective-permute-start | bytes 1769480 | tf_op jit(solution)/shard_map/ppermute | solution.py:839
  57.7 5.4 %collective-permute-start.4 = (f32[288,512]{1,0:T(8,128)}, f32[288,512]{1,0:T(8,128)}, u32[]{:S(2)}, u32[]{:S(2)}) collective-permute-start(f32[288,512]{1,0:T(8,128)} %get-tuple-element.64), channel_id=1, source_target_pairs={{0,4},{4,8},{8,12},{12,16},{16,20},{20,24},{24,28},{1,5},{5,9},{9,... | collective-permute-start | bytes 1769480 | tf_op jit(solution)/shard_map/ppermute | solution.py:838
  63.1 1.6 %all-to-all-done.2 = f32[32,16,128]{2,1,0:T(8,128)} async-done(((f32[32,16,128]{2,1,0:T(8,128)}), f32[32,16,128]{2,1,0:T(8,128)}, u32[]{:S(2)}, u32[]{:S(2)}) %all-to-all-start.2) | async-done | bytes 262176 | tf_op jit(solution)/shard_map/all_to_all | solution.py:827
  64.7 7.7 %tiles.3 = f32[512,128]{1,0:T(8,128)} custom-call(s32[1]{0:T(128)S(6)} %copy.11.live_ref, s32[2,256]{1,0:T(2,128)} %bitcast.9, s32[2,256]{1,0:T(2,128)} %bitcast.10, f32[512,128]{1,0:T(8,128)} %bitcast.3.whole_ref, f32[256,128,128]{2,1,0:T(8,128)} %tiles_ref.3), custom_call_target="tpu_custom_call" | custom-call | flops 134217728 | bytes 16777216 | tf_op jit(solution)/shard_map/tiles/pallas_call | solution.py:200
  72.4 6.0 %all-to-all-start.3 = ((f32[32,16,128]{2,1,0:T(8,128)}), f32[32,16,128]{2,1,0:T(8,128)}, u32[]{:S(2)}, u32[]{:S(2)}) async-start(f32[32,16,128]{2,1,0:T(8,128)} %bitcast.6), calls=%async_computation.3 | async-start | bytes 524288 | tf_op jit(solution)/shard_map/all_to_all | solution.py:827
  78.4 7.9 %own_planes.1 = (f32[16,72,512]{2,1,0:T(8,128)}, f32[16,72,512]{2,1,0:T(8,128)}, f32[16,72,512]{2,1,0:T(8,128)}, f32[16,8,128]{2,1,0:T(8,128)}) custom-call(f32[16,64,512]{2,1,0:T(8,128)} %t_ref, f32[16,64,512]{2,1,0:T(8,128)} %k_ref, f32[16,8,512]{2,1,0:T(8,128)} %collective-permute-done.below0.below1.below_ref, ...), custom_call_target="tpu_custom_call" | custom-call | flops 5898240 | bytes 14155776 | tf_op jit(solution)/shard_map/own_planes/pallas_call | solution.py:579
  86.4 0.0 collective-permute-done.5.t_high
  86.4 3.6 %collective-permute-done.4.t_low = f32[288,512]{1,0:T(8,128)} collective-permute-done((f32[288,512]{1,0:T(8,128)}, f32[288,512]{1,0:T(8,128)}, u32[]{:S(2)}, u32[]{:S(2)}) %collective-permute-start.4) | collective-permute-done | bytes 589856 | tf_op jit(solution)/shard_map/ppermute | solution.py:838
  90.0 0.2 all-to-all-done.3.parts_ref
  90.1 2.2 %last.1 = (f32[16,128]{1,0:T(8,128)}, f32[32,8,128]{2,1,0:T(8,128)}) custom-call(f32[32,16,128]{2,1,0:T(8,128)} %all-to-all-done.3.parts_ref, f32[16,128]{1,0:T(8,128)} %get-tuple-element.57.emitted_ref, f32[16,128]{1,0:T(8,128)} %mirror_ref.5, s32[16,128]{1,0:T(8,128)} %site_ref.3), custom_call_target="tpu_custom_call" | custom-call | flops 10000000 | bytes 600000 | tf_op jit(solution)/shard_map/last/pallas_call | solution.py:273
  92.3 5.1 %all-to-all-start.4 = ((f32[32,8,128]{2,1,0:T(8,128)}), f32[32,8,128]{2,1,0:T(8,128)}, u32[]{:S(2)}, u32[]{:S(2)}) async-start(f32[32,8,128]{2,1,0:T(8,128)} %get-tuple-element.75), calls=%async_computation.4 | async-start | bytes 262144 | tf_op jit(solution)/shard_map/all_to_all | solution.py:827
  97.4 21.0 %heat.1 = (f32[16,64,512]{2,1,0:T(8,128)}, f32[24,8,128]{2,1,0:T(8,128)}) custom-call(f32[16,72,512]{2,1,0:T(8,128)} %get-tuple-element.80.own_field, f32[16,72,512]{2,1,0:T(8,128)} %get-tuple-element.81.own_faces, f32[16,72,512]{2,1,0:T(8,128)} %get-tuple-element.82.own_gz, f32[16,8,128]{2,1,0:T(8,128)} %get-tuple-element.83.own_thin, ...), custom_call_target="tpu_custom_call" | custom-call | flops 88473600 | bytes 25165824 | tf_op jit(solution)/shard_map/heat/pallas_call | solution.py:700
  118.4 0.0 all-to-all-done.4.all_ref
  118.4 2.6 %add_source.1 = f32[16,64,512]{2,1,0:T(8,128)} custom-call(f32[32,8,128]{2,1,0:T(8,128)} %all-to-all-done.4.all_ref, f32[24,8,128]{2,1,0:T(8,128)} %get-tuple-element.88.thin_ref, f32[16,64,512]{2,1,0:T(8,128)} %get-tuple-element.89.base_ref), custom_call_target="tpu_custom_call", output_to_operand_aliasing={{}: (2, {})} | custom-call | flops 1000000 | bytes 1048576 | tf_op jit(solution)/shard_map/add_source/pallas_call | solution.py:809
Async XLA Ops:
  2.8 18.0 %all-to-all-start = ((f32[32,16,128]{2,1,0:T(8,128)}), f32[32,16,128]{2,1,0:T(8,128)}, u32[]{:S(2)}, u32[]{:S(2)}) async-start(f32[32,16,128]{2,1,0:T(8,128)} %get-tuple-element.48), calls=%async_computation | async-start | bytes 524288 | tf_op jit(solution)/shard_map/all_to_all | solution.py:827
  12.5 29.4 %collective-permute-start.2 = (f32[4,64,512]{2,1,0:T(8,128)}, f32[4,64,512]{2,1,0:T(8,128)}, u32[]{:S(2)}, u32[]{:S(2)}) collective-permute-start(f32[4,64,512]{2,1,0:T(8,128)} %get-tuple-element.90), channel_id=1, source_target_pairs={{0,4},{4,8},{8,12},{12,16},{16,20},{20,24},{24,28},{1,5},{5,9},{9,... | collective-permute-start | bytes 1572872 | tf_op jit(solution)/shard_map/ppermute | solution.py:838
  16.9 25.0 %collective-permute-start.3 = (f32[4,64,512]{2,1,0:T(8,128)}, f32[4,64,512]{2,1,0:T(8,128)}, u32[]{:S(2)}, u32[]{:S(2)}) collective-permute-start(f32[4,64,512]{2,1,0:T(8,128)} %get-tuple-element.91), channel_id=1, source_target_pairs={{4,0},{8,4},{12,8},{16,12},{20,16},{24,20},{28,24},{5,1},{9,5},{13... | collective-permute-start | bytes 1572872 | tf_op jit(solution)/shard_map/ppermute | solution.py:839
  28.5 16.3 %all-to-all-start.1 = ((f32[32,16,128]{2,1,0:T(8,128)}), f32[32,16,128]{2,1,0:T(8,128)}, u32[]{:S(2)}, u32[]{:S(2)}) async-start(f32[32,16,128]{2,1,0:T(8,128)} %bitcast.5), calls=%async_computation.1 | async-start | bytes 524288 | tf_op jit(solution)/shard_map/all_to_all | solution.py:827
  36.3 5.6 %collective-permute-start = (f32[16,8,512]{2,1,0:T(8,128)}, f32[16,8,512]{2,1,0:T(8,128)}, u32[]{:S(2)}, u32[]{:S(2)}) collective-permute-start(f32[16,8,512]{2,1,0:T(8,128)} %get-tuple-element.54), channel_id=1, source_target_pairs={{0,1},{1,2},{2,3},{4,5},{5,6},{6,7},{8,9},{9,10},{10,11},{12,13},{... | collective-permute-start | bytes 786440 | tf_op jit(solution)/shard_map/ppermute | solution.py:838
  39.0 4.2 %collective-permute-start.1 = (f32[16,8,512]{2,1,0:T(8,128)}, f32[16,8,512]{2,1,0:T(8,128)}, u32[]{:S(2)}, u32[]{:S(2)}) collective-permute-start(f32[16,8,512]{2,1,0:T(8,128)} %get-tuple-element.55), channel_id=1, source_target_pairs={{1,0},{2,1},{3,2},{5,4},{6,5},{7,6},{9,8},{10,9},{11,10},{13,12},{... | collective-permute-start | bytes 786440 | tf_op jit(solution)/shard_map/ppermute | solution.py:839
  46.5 18.1 %all-to-all-start.2 = ((f32[32,16,128]{2,1,0:T(8,128)}), f32[32,16,128]{2,1,0:T(8,128)}, u32[]{:S(2)}, u32[]{:S(2)}) async-start(f32[32,16,128]{2,1,0:T(8,128)} %middle.1), calls=%async_computation.2 | async-start | bytes 524288 | tf_op jit(solution)/shard_map/all_to_all | solution.py:827
  56.4 30.0 %collective-permute-start.5 = (f32[288,512]{1,0:T(8,128)}, f32[288,512]{1,0:T(8,128)}, u32[]{:S(2)}, u32[]{:S(2)}) collective-permute-start(f32[288,512]{1,0:T(8,128)} %get-tuple-element.63), channel_id=1, source_target_pairs={{4,0},{8,4},{12,8},{16,12},{20,16},{24,20},{28,24},{5,1},{9,5},{13... | collective-permute-start | bytes 1769480 | tf_op jit(solution)/shard_map/ppermute | solution.py:839
  57.7 32.3 %collective-permute-start.4 = (f32[288,512]{1,0:T(8,128)}, f32[288,512]{1,0:T(8,128)}, u32[]{:S(2)}, u32[]{:S(2)}) collective-permute-start(f32[288,512]{1,0:T(8,128)} %get-tuple-element.64), channel_id=1, source_target_pairs={{0,4},{4,8},{8,12},{12,16},{16,20},{20,24},{24,28},{1,5},{5,9},{9,... | collective-permute-start | bytes 1769480 | tf_op jit(solution)/shard_map/ppermute | solution.py:838
  72.4 17.7 %all-to-all-start.3 = ((f32[32,16,128]{2,1,0:T(8,128)}), f32[32,16,128]{2,1,0:T(8,128)}, u32[]{:S(2)}, u32[]{:S(2)}) async-start(f32[32,16,128]{2,1,0:T(8,128)} %bitcast.6), calls=%async_computation.3 | async-start | bytes 524288 | tf_op jit(solution)/shard_map/all_to_all | solution.py:827
  92.3 26.1 %all-to-all-start.4 = ((f32[32,8,128]{2,1,0:T(8,128)}), f32[32,8,128]{2,1,0:T(8,128)}, u32[]{:S(2)}, u32[]{:S(2)}) async-start(f32[32,8,128]{2,1,0:T(8,128)} %get-tuple-element.75), calls=%async_computation.4 | async-start | bytes 262144 | tf_op jit(solution)/shard_map/all_to_all | solution.py:827

commit v2 on v1

--- a/solution.py
+++ b/solution.py
@@ -592,7 +592,7 @@
 
 def heat_kernel(
     own_field, own_faces, own_gz, own_thin, k_low, k_high, t_low, t_high, out_ref, thin_ref,
-    loaded, corners, field, between, faces, gz, placed, sems, own_sems,
+    loaded, corners, field, between, faces, gz, placed, sems, own_sems, out_sems,
 ):
     nx, wide, nz = own_field.shape
     ny = wide - 2 * ROWS
@@ -683,12 +683,20 @@
                 new[x] = jnp.zeros((wide, nz), jnp.float32)
 
         old, new = new, old
-    one_step(old, faces, gz, HALO, tall - HALO, outside)
-
-    @pl.loop(0, nx)
-    def _(x):
-        for j, z in enumerate(spans):
-            out_ref[x, :, z] = placed[x, j, :ny, :]
+    results = []
+    for part, begin in enumerate((0, nx // 2)):
+        planes = nx // 2
+        one_step(old, faces, gz, HALO + begin, HALO + begin + planes, outside)
+        for j in range(len(spans)):
+            copy = pltpu.make_async_copy(
+                placed.at[pl.ds(begin, planes), j, pl.ds(0, ny)],
+                out_ref.at[pl.ds(begin, planes), :, pl.ds(j * LANES, LANES)],
+                out_sems.at[part, j],
+            )
+            copy.start()
+            results.append(copy)
+    for copy in results:
+        copy.wait()
 
 
 def heat(own, k_low, k_high, t_low, t_high, shape):
@@ -704,6 +712,7 @@
             jax.ShapeDtypeStruct((tall, 8, LANES), jnp.float32),
         ),
         in_specs=[hbm] * 3 + [vmem] + [hbm] * 4,
+        out_specs=(hbm, vmem),
         scratch_shapes=[
             pltpu.VMEM((2, 2 * HALO, nz // LANES, wide, LANES), jnp.float32),
             pltpu.VMEM((2, 32, nz), jnp.float32),
@@ -714,6 +723,7 @@
             pltpu.VMEM((nx, nz // LANES, wide, LANES), jnp.float32),
             pltpu.SemaphoreType.DMA((6 * HALO, nz // LANES)),
             pltpu.SemaphoreType.DMA((5,)),
+            pltpu.SemaphoreType.DMA((2, nz // LANES)),
         ],
         compiler_params=params(64),
         cost_estimate=cost(tall * wide * nz * 100, 12 * nx * ny * nz * 4),

time: 122 us -> 123 us (level)
  starting transfers between devices: 48.2 us -> 53 us
  Pallas kernels: 57.4 us -> 54.3 us
    all_to_all x5, starting transfers between devices: 31.8 us -> 36.7 us  [exchange(): lax.all_to_all(rows, ('slab', 'pair'), split_axis=0, concat_axis=0, tiled...]
    pallas_call x2, Pallas kernels: 15.5 us -> 12.2 us  [tile_terms(): pl.pallas_call(tiles_kernel, out_shape=jax.ShapeDtypeStruct(whole.shape,...]
    ppermute x3, waiting for transfers between devices: 1.35 us -> 2.9 us  [both_ways(): from_high = lax.ppermute(low, axis, backward)]
    ppermute x3, waiting for transfers between devices: 5.16 us -> 3.67 us  [both_ways(): from_low = lax.ppermute(high, axis, forward)]
  transfers between devices with their start and end apart: 11 -> 11, of which waited for: 7 -> 6; matrix products, arithmetic and copies ran while one was open for 2% -> 2% of each run, Pallas kernels for 40% -> 37%
where the time goes in v2:
time: 123 us
  Pallas kernels  54.3 us (44%)
  starting transfers between devices  53 us (43%)
  waiting for transfers between devices  11.8 us (10%)
  local copies, waits for them, and re-layouts  2.25 us (2%)
  between operations  1.42 us (1%)
    all_to_all x5, starting transfers between devices, exchange(): lax.all_to_all(rows, ('slab', 'pair'), split_axis=0, concat_axis=0, tiled...  36.7 us
    pallas_call x1, Pallas kernels, heat(): pl.pallas_call(heat_kernel, out_shape=(jax.ShapeDtypeStruct(shape, jnp.fl...  21.2 us
    ppermute x3, starting transfers between devices, both_ways(): from_low = lax.ppermute(high, axis, forward)  12.6 us
    pallas_call x2, Pallas kernels, tile_terms(): pl.pallas_call(tiles_kernel, out_shape=jax.ShapeDtypeStruct(whole.shape,...  12.2 us
    pallas_call x1, Pallas kernels, own_planes(): pl.pallas_call(own_planes_kernel, out_shape=(shape, shape, shape, jax.Sha...  7.93 us
    all_to_all x5, waiting for transfers between devices, exchange(): lax.all_to_all(rows, ('slab', 'pair'), split_axis=0, concat_axis=0, tiled...  5.25 us
    ppermute x3, starting transfers between devices, both_ways(): from_high = lax.ppermute(low, axis, backward)  3.84 us
    ppermute x3, waiting for transfers between devices, both_ways(): from_low = lax.ppermute(high, axis, forward)  3.67 us
  transfers between devices with their start and end apart: 11, of which 6 were waited for; matrix products, arithmetic and copies ran while one was open for 2% of the time, Pallas kernels for 37%

profile of v2, /device:TPU:0, one launch (start us, length us, event | category | flops | bytes accessed | tf_op | source)
XLA Modules:
  0.0 122.9 jit_solution(6685279492010572931)
XLA Ops:
  0.6 2.1 %emit.1 = (f32[16,128]{1,0:T(8,128)}, f32[32,16,128]{2,1,0:T(8,128)}) custom-call(f32[16,64,512]{2,1,0:T(8,128)} %t_ref, s32[16,128]{1,0:T(8,128)} %site_ref.3, f32[16,128]{1,0:T(8,128)} %mirror_ref.5), custom_call_target="tpu_custom_call" | custom-call | flops 10000 | bytes 900000 | tf_op jit(solution)/shard_map/emit/pallas_call | solution.py:96
  2.8 7.4 %all-to-all-start = ((f32[32,16,128]{2,1,0:T(8,128)}), f32[32,16,128]{2,1,0:T(8,128)}, u32[]{:S(2)}, u32[]{:S(2)}) async-start(f32[32,16,128]{2,1,0:T(8,128)} %get-tuple-element.48), calls=%async_computation | async-start | bytes 524288 | tf_op jit(solution)/shard_map/all_to_all | solution.py:837
  10.2 2.3 %fusion = (f32[4,64,512]{2,1,0:T(8,128)}, f32[4,64,512]{2,1,0:T(8,128)}) fusion(f32[16,64,512]{2,1,0:T(8,128)} %k_ref), kind=kLoop, calls=%fused_computation | loop fusion | bytes 2097152 | tf_op jit(solution)/shard_map/slice | solution.py:879
  12.5 4.4 %collective-permute-start.2 = (f32[4,64,512]{2,1,0:T(8,128)}, f32[4,64,512]{2,1,0:T(8,128)}, u32[]{:S(2)}, u32[]{:S(2)}) collective-permute-start(f32[4,64,512]{2,1,0:T(8,128)} %get-tuple-element.90), channel_id=1, source_target_pairs={{0,4},{4,8},{8,12},{12,16},{16,20},{20,24},{24,28},{1,5},{5,9},{9,... | collective-permute-start | bytes 1572872 | tf_op jit(solution)/shard_map/ppermute | solution.py:848
  16.9 1.3 %collective-permute-start.3 = (f32[4,64,512]{2,1,0:T(8,128)}, f32[4,64,512]{2,1,0:T(8,128)}, u32[]{:S(2)}, u32[]{:S(2)}) collective-permute-start(f32[4,64,512]{2,1,0:T(8,128)} %get-tuple-element.91), channel_id=1, source_target_pairs={{4,0},{8,4},{12,8},{16,12},{20,16},{24,20},{28,24},{5,1},{9,5},{13... | collective-permute-start | bytes 1572872 | tf_op jit(solution)/shard_map/ppermute | solution.py:849
  18.8 2.0 %all-to-all-done = f32[32,16,128]{2,1,0:T(8,128)} async-done(((f32[32,16,128]{2,1,0:T(8,128)}), f32[32,16,128]{2,1,0:T(8,128)}, u32[]{:S(2)}, u32[]{:S(2)}) %all-to-all-start) | async-done | bytes 262176 | tf_op jit(solution)/shard_map/all_to_all | solution.py:837
  20.8 6.1 %tiles.2 = f32[512,128]{1,0:T(8,128)} custom-call(s32[1]{0:T(128)S(6)} %copy.11.live_ref, s32[2,256]{1,0:T(2,128)} %bitcast.7, s32[2,256]{1,0:T(2,128)} %bitcast.8, f32[512,128]{1,0:T(8,128)} %bitcast.1.whole_ref, f32[256,128,128]{2,1,0:T(8,128)} %tiles_ref.3), custom_call_target="tpu_custom_call" | custom-call | flops 134217728 | bytes 16777216 | tf_op jit(solution)/shard_map/tiles/pallas_call | solution.py:200
  26.9 9.0 %all-to-all-start.1 = ((f32[32,16,128]{2,1,0:T(8,128)}), f32[32,16,128]{2,1,0:T(8,128)}, u32[]{:S(2)}, u32[]{:S(2)}) async-start(f32[32,16,128]{2,1,0:T(8,128)} %bitcast.5), calls=%async_computation.1 | async-start | bytes 524288 | tf_op jit(solution)/shard_map/all_to_all | solution.py:837
  35.9 2.0 %pack_y.1 = (f32[16,8,512]{2,1,0:T(8,128)}, f32[16,8,512]{2,1,0:T(8,128)}) custom-call(f32[16,64,512]{2,1,0:T(8,128)} %t_ref, f32[16,64,512]{2,1,0:T(8,128)} %k_ref, f32[16,64,512]{2,1,0:T(8,128)} %t_ref, f32[16,64,512]{2,1,0:T(8,128)} %k_ref), custom_call_target="tpu_custom_call" | custom-call | bytes 1048576 | tf_op jit(solution)/shard_map/pack_y/pallas_call | solution.py:297
  38.0 2.8 %collective-permute-start = (f32[16,8,512]{2,1,0:T(8,128)}, f32[16,8,512]{2,1,0:T(8,128)}, u32[]{:S(2)}, u32[]{:S(2)}) collective-permute-start(f32[16,8,512]{2,1,0:T(8,128)} %get-tuple-element.54), channel_id=1, source_target_pairs={{0,1},{1,2},{2,3},{4,5},{5,6},{6,7},{8,9},{9,10},{10,11},{12,13},{... | collective-permute-start | bytes 786440 | tf_op jit(solution)/shard_map/ppermute | solution.py:848
  40.7 1.3 %collective-permute-start.1 = (f32[16,8,512]{2,1,0:T(8,128)}, f32[16,8,512]{2,1,0:T(8,128)}, u32[]{:S(2)}, u32[]{:S(2)}) collective-permute-start(f32[16,8,512]{2,1,0:T(8,128)} %get-tuple-element.55), channel_id=1, source_target_pairs={{1,0},{2,1},{3,2},{5,4},{6,5},{7,6},{9,8},{10,9},{11,10},{13,12},{... | collective-permute-start | bytes 786440 | tf_op jit(solution)/shard_map/ppermute | solution.py:849
  42.0 0.0 collective-permute-done.2.k_low
  42.0 0.0 collective-permute-done.3.k_high
  42.1 0.0 collective-permute-done.below0.below1.below_ref
  42.1 2.9 %collective-permute-done.1.above0.above1.above_ref = f32[16,8,512]{2,1,0:T(8,128)} collective-permute-done((f32[16,8,512]{2,1,0:T(8,128)}, f32[16,8,512]{2,1,0:T(8,128)}, u32[]{:S(2)}, u32[]{:S(2)}) %collective-permute-start.1) | collective-permute-done | bytes 262176 | tf_op jit(solution)/shard_map/ppermute | solution.py:849
  45.0 1.5 %all-to-all-done.1.parts_ref = f32[32,16,128]{2,1,0:T(8,128)} async-done(((f32[32,16,128]{2,1,0:T(8,128)}), f32[32,16,128]{2,1,0:T(8,128)}, u32[]{:S(2)}, u32[]{:S(2)}) %all-to-all-start.1) | async-done | bytes 262176 | tf_op jit(solution)/shard_map/all_to_all | solution.py:837
  46.5 1.7 %middle.1 = f32[32,16,128]{2,1,0:T(8,128)} custom-call(f32[32,16,128]{2,1,0:T(8,128)} %all-to-all-done.1.parts_ref, f32[16,128]{1,0:T(8,128)} %get-tuple-element.57.emitted_ref, f32[16,128]{1,0:T(8,128)} %mirror_ref.5), custom_call_target="tpu_custom_call" | custom-call | flops 100000 | bytes 600000 | tf_op jit(solution)/shard_map/middle/pallas_call | solution.py:233
  48.2 7.6 %all-to-all-start.2 = ((f32[32,16,128]{2,1,0:T(8,128)}), f32[32,16,128]{2,1,0:T(8,128)}, u32[]{:S(2)}, u32[]{:S(2)}) async-start(f32[32,16,128]{2,1,0:T(8,128)} %middle.1), calls=%async_computation.2 | async-start | bytes 524288 | tf_op jit(solution)/shard_map/all_to_all | solution.py:837
  55.8 2.3 %pack_x.1 = (f32[288,512]{1,0:T(8,128)}, f32[288,512]{1,0:T(8,128)}) custom-call(f32[16,64,512]{2,1,0:T(8,128)} %t_ref, f32[16,64,512]{2,1,0:T(8,128)} %t_ref, f32[16,8,512]{2,1,0:T(8,128)} %collective-permute-done.below0.below1.below_ref, f32[16,8,512]{2,1,0:T(8,128)} %collective-permute-done.1.above0.above1.above_ref, ...), custom_call_target="tpu_custom_call" | custom-call | bytes 2359296 | tf_op jit(solution)/shard_map/pack_x/pallas_call | solution.py:357
  58.1 1.3 %collective-permute-start.5 = (f32[288,512]{1,0:T(8,128)}, f32[288,512]{1,0:T(8,128)}, u32[]{:S(2)}, u32[]{:S(2)}) collective-permute-start(f32[288,512]{1,0:T(8,128)} %get-tuple-element.63), channel_id=1, source_target_pairs={{4,0},{8,4},{12,8},{16,12},{20,16},{24,20},{28,24},{5,1},{9,5},{13... | collective-permute-start | bytes 1769480 | tf_op jit(solution)/shard_map/ppermute | solution.py:849
  59.4 5.4 %collective-permute-start.4 = (f32[288,512]{1,0:T(8,128)}, f32[288,512]{1,0:T(8,128)}, u32[]{:S(2)}, u32[]{:S(2)}) collective-permute-start(f32[288,512]{1,0:T(8,128)} %get-tuple-element.64), channel_id=1, source_target_pairs={{0,4},{4,8},{8,12},{12,16},{16,20},{20,24},{24,28},{1,5},{5,9},{9,... | collective-permute-start | bytes 1769480 | tf_op jit(solution)/shard_map/ppermute | solution.py:848
  64.8 1.6 %all-to-all-done.2 = f32[32,16,128]{2,1,0:T(8,128)} async-done(((f32[32,16,128]{2,1,0:T(8,128)}), f32[32,16,128]{2,1,0:T(8,128)}, u32[]{:S(2)}, u32[]{:S(2)}) %all-to-all-start.2) | async-done | bytes 262176 | tf_op jit(solution)/shard_map/all_to_all | solution.py:837
  66.4 6.1 %tiles.3 = f32[512,128]{1,0:T(8,128)} custom-call(s32[1]{0:T(128)S(6)} %copy.11.live_ref, s32[2,256]{1,0:T(2,128)} %bitcast.9, s32[2,256]{1,0:T(2,128)} %bitcast.10, f32[512,128]{1,0:T(8,128)} %bitcast.3.whole_ref, f32[256,128,128]{2,1,0:T(8,128)} %tiles_ref.3), custom_call_target="tpu_custom_call" | custom-call | flops 134217728 | bytes 16777216 | tf_op jit(solution)/shard_map/tiles/pallas_call | solution.py:200
  72.5 7.6 %all-to-all-start.3 = ((f32[32,16,128]{2,1,0:T(8,128)}), f32[32,16,128]{2,1,0:T(8,128)}, u32[]{:S(2)}, u32[]{:S(2)}) async-start(f32[32,16,128]{2,1,0:T(8,128)} %bitcast.6), calls=%async_computation.3 | async-start | bytes 524288 | tf_op jit(solution)/shard_map/all_to_all | solution.py:837
  80.1 7.9 %own_planes.1 = (f32[16,72,512]{2,1,0:T(8,128)}, f32[16,72,512]{2,1,0:T(8,128)}, f32[16,72,512]{2,1,0:T(8,128)}, f32[16,8,128]{2,1,0:T(8,128)}) custom-call(f32[16,64,512]{2,1,0:T(8,128)} %t_ref, f32[16,64,512]{2,1,0:T(8,128)} %k_ref, f32[16,8,512]{2,1,0:T(8,128)} %collective-permute-done.below0.below1.below_ref, ...), custom_call_target="tpu_custom_call" | custom-call | flops 5898240 | bytes 14155776 | tf_op jit(solution)/shard_map/own_planes/pallas_call | solution.py:579
  88.0 0.0 collective-permute-done.5.t_high
  88.0 3.7 %collective-permute-done.4.t_low = f32[288,512]{1,0:T(8,128)} collective-permute-done((f32[288,512]{1,0:T(8,128)}, f32[288,512]{1,0:T(8,128)}, u32[]{:S(2)}, u32[]{:S(2)}) %collective-permute-start.4) | collective-permute-done | bytes 589856 | tf_op jit(solution)/shard_map/ppermute | solution.py:848
  91.7 0.2 all-to-all-done.3.parts_ref
  91.8 2.2 %last.1 = (f32[16,128]{1,0:T(8,128)}, f32[32,8,128]{2,1,0:T(8,128)}) custom-call(f32[32,16,128]{2,1,0:T(8,128)} %all-to-all-done.3.parts_ref, f32[16,128]{1,0:T(8,128)} %get-tuple-element.57.emitted_ref, f32[16,128]{1,0:T(8,128)} %mirror_ref.5, s32[16,128]{1,0:T(8,128)} %site_ref.3), custom_call_target="tpu_custom_call" | custom-call | flops 10000000 | bytes 600000 | tf_op jit(solution)/shard_map/last/pallas_call | solution.py:273
  94.0 5.1 %all-to-all-start.4 = ((f32[32,8,128]{2,1,0:T(8,128)}), f32[32,8,128]{2,1,0:T(8,128)}, u32[]{:S(2)}, u32[]{:S(2)}) async-start(f32[32,8,128]{2,1,0:T(8,128)} %get-tuple-element.75), calls=%async_computation.4 | async-start | bytes 262144 | tf_op jit(solution)/shard_map/all_to_all | solution.py:837
  99.1 21.2 %heat.1 = (f32[16,64,512]{2,1,0:T(8,128)}, f32[24,8,128]{2,1,0:T(8,128)}) custom-call(f32[16,72,512]{2,1,0:T(8,128)} %get-tuple-element.80.own_field, f32[16,72,512]{2,1,0:T(8,128)} %get-tuple-element.81.own_faces, f32[16,72,512]{2,1,0:T(8,128)} %get-tuple-element.82.own_gz, f32[16,8,128]{2,1,0:T(8,128)} %get-tuple-element.83.own_thin, ...), custom_call_target="tpu_custom_call" | custom-call | flops 88473600 | bytes 25165824 | tf_op jit(solution)/shard_map/heat/pallas_call | solution.py:708
  120.3 0.0 all-to-all-done.4.all_ref
  120.3 2.6 %add_source.1 = f32[16,64,512]{2,1,0:T(8,128)} custom-call(f32[32,8,128]{2,1,0:T(8,128)} %all-to-all-done.4.all_ref, f32[24,8,128]{2,1,0:T(8,128)} %get-tuple-element.88.thin_ref, f32[16,64,512]{2,1,0:T(8,128)} %get-tuple-element.89.base_ref), custom_call_target="tpu_custom_call", output_to_operand_aliasing={{}: (2, {})} | custom-call | flops 1000000 | bytes 1048576 | tf_op jit(solution)/shard_map/add_source/pallas_call | solution.py:819
Async XLA Ops:
  2.8 18.0 %all-to-all-start = ((f32[32,16,128]{2,1,0:T(8,128)}), f32[32,16,128]{2,1,0:T(8,128)}, u32[]{:S(2)}, u32[]{:S(2)}) async-start(f32[32,16,128]{2,1,0:T(8,128)} %get-tuple-element.48), calls=%async_computation | async-start | bytes 524288 | tf_op jit(solution)/shard_map/all_to_all | solution.py:837
  12.5 29.6 %collective-permute-start.2 = (f32[4,64,512]{2,1,0:T(8,128)}, f32[4,64,512]{2,1,0:T(8,128)}, u32[]{:S(2)}, u32[]{:S(2)}) collective-permute-start(f32[4,64,512]{2,1,0:T(8,128)} %get-tuple-element.90), channel_id=1, source_target_pairs={{0,4},{4,8},{8,12},{12,16},{16,20},{20,24},{24,28},{1,5},{5,9},{9,... | collective-permute-start | bytes 1572872 | tf_op jit(solution)/shard_map/ppermute | solution.py:848
  16.9 25.2 %collective-permute-start.3 = (f32[4,64,512]{2,1,0:T(8,128)}, f32[4,64,512]{2,1,0:T(8,128)}, u32[]{:S(2)}, u32[]{:S(2)}) collective-permute-start(f32[4,64,512]{2,1,0:T(8,128)} %get-tuple-element.91), channel_id=1, source_target_pairs={{4,0},{8,4},{12,8},{16,12},{20,16},{24,20},{28,24},{5,1},{9,5},{13... | collective-permute-start | bytes 1572872 | tf_op jit(solution)/shard_map/ppermute | solution.py:849
  26.9 19.6 %all-to-all-start.1 = ((f32[32,16,128]{2,1,0:T(8,128)}), f32[32,16,128]{2,1,0:T(8,128)}, u32[]{:S(2)}, u32[]{:S(2)}) async-start(f32[32,16,128]{2,1,0:T(8,128)} %bitcast.5), calls=%async_computation.1 | async-start | bytes 524288 | tf_op jit(solution)/shard_map/all_to_all | solution.py:837
  38.0 4.1 %collective-permute-start = (f32[16,8,512]{2,1,0:T(8,128)}, f32[16,8,512]{2,1,0:T(8,128)}, u32[]{:S(2)}, u32[]{:S(2)}) collective-permute-start(f32[16,8,512]{2,1,0:T(8,128)} %get-tuple-element.54), channel_id=1, source_target_pairs={{0,1},{1,2},{2,3},{4,5},{5,6},{6,7},{8,9},{9,10},{10,11},{12,13},{... | collective-permute-start | bytes 786440 | tf_op jit(solution)/shard_map/ppermute | solution.py:848
  40.7 4.2 %collective-permute-start.1 = (f32[16,8,512]{2,1,0:T(8,128)}, f32[16,8,512]{2,1,0:T(8,128)}, u32[]{:S(2)}, u32[]{:S(2)}) collective-permute-start(f32[16,8,512]{2,1,0:T(8,128)} %get-tuple-element.55), channel_id=1, source_target_pairs={{1,0},{2,1},{3,2},{5,4},{6,5},{7,6},{9,8},{10,9},{11,10},{13,12},{... | collective-permute-start | bytes 786440 | tf_op jit(solution)/shard_map/ppermute | solution.py:849
  48.2 18.1 %all-to-all-start.2 = ((f32[32,16,128]{2,1,0:T(8,128)}), f32[32,16,128]{2,1,0:T(8,128)}, u32[]{:S(2)}, u32[]{:S(2)}) async-start(f32[32,16,128]{2,1,0:T(8,128)} %middle.1), calls=%async_computation.2 | async-start | bytes 524288 | tf_op jit(solution)/shard_map/all_to_all | solution.py:837
  58.1 29.9 %collective-permute-start.5 = (f32[288,512]{1,0:T(8,128)}, f32[288,512]{1,0:T(8,128)}, u32[]{:S(2)}, u32[]{:S(2)}) collective-permute-start(f32[288,512]{1,0:T(8,128)} %get-tuple-element.63), channel_id=1, source_target_pairs={{4,0},{8,4},{12,8},{16,12},{20,16},{24,20},{28,24},{5,1},{9,5},{13... | collective-permute-start | bytes 1769480 | tf_op jit(solution)/shard_map/ppermute | solution.py:849
  59.4 32.3 %collective-permute-start.4 = (f32[288,512]{1,0:T(8,128)}, f32[288,512]{1,0:T(8,128)}, u32[]{:S(2)}, u32[]{:S(2)}) collective-permute-start(f32[288,512]{1,0:T(8,128)} %get-tuple-element.64), channel_id=1, source_target_pairs={{0,4},{4,8},{8,12},{12,16},{16,20},{20,24},{24,28},{1,5},{5,9},{9,... | collective-permute-start | bytes 1769480 | tf_op jit(solution)/shard_map/ppermute | solution.py:848
  72.5 19.4 %all-to-all-start.3 = ((f32[32,16,128]{2,1,0:T(8,128)}), f32[32,16,128]{2,1,0:T(8,128)}, u32[]{:S(2)}, u32[]{:S(2)}) async-start(f32[32,16,128]{2,1,0:T(8,128)} %bitcast.6), calls=%async_computation.3 | async-start | bytes 524288 | tf_op jit(solution)/shard_map/all_to_all | solution.py:837
  94.0 26.3 %all-to-all-start.4 = ((f32[32,8,128]{2,1,0:T(8,128)}), f32[32,8,128]{2,1,0:T(8,128)}, u32[]{:S(2)}, u32[]{:S(2)}) async-start(f32[32,8,128]{2,1,0:T(8,128)} %get-tuple-element.75), calls=%async_computation.4 | async-start | bytes 262144 | tf_op jit(solution)/shard_map/all_to_all | solution.py:837

commit v3 on v1

--- a/solution.py
+++ b/solution.py
@@ -592,9 +592,10 @@
 
 def heat_kernel(
     own_field, own_faces, own_gz, own_thin, k_low, k_high, t_low, t_high, out_ref, thin_ref,
-    loaded, corners, field, between, faces, gz, placed, sems, own_sems,
+    loaded, corners, fields, faces, gz, placed, sems, own_sems,
 ):
     nx, wide, nz = own_field.shape
+    field = fields.at[0]
     ny = wide - 2 * ROWS
     tall = nx + 2 * HALO
     tiles = wide // 8
@@ -667,22 +668,24 @@
     def _():
         faces[HALO + nx] = faces[HALO + nx - 1]
 
-    def inside(target):
-        return lambda x, t, z: (target, (x, slice(8 * t, 8 * t + 8), z))
-
     def outside(x, t, z):
         return placed, (x - HALO, z.start // LANES, pl.ds(t, 8, stride=tiles))
 
-    old, new = field, between
-    for step in range(1, STEPS):
-        one_step(old, faces, gz, step, tall - step, inside(new))
+    @pl.loop(1, STEPS)
+    def _(step):
+        old, new = (step - 1) & 1, step & 1
+
+        def inside(x, t, z):
+            return fields, (new, x, slice(8 * t, 8 * t + 8), z)
+
+        one_step(fields.at[old], faces, gz, step, tall - step, inside)
         for x, there in ((HALO - 1, has_low), (HALO + nx, has_high)):
 
             @pl.when(jnp.logical_not(there))
             def _():
-                new[x] = jnp.zeros((wide, nz), jnp.float32)
-
-        old, new = new, old
+                fields[new, x] = jnp.zeros((wide, nz), jnp.float32)
+
+    old = fields.at[(STEPS - 1) & 1]
     one_step(old, faces, gz, HALO, tall - HALO, outside)
 
     @pl.loop(0, nx)
@@ -707,8 +710,7 @@
         scratch_shapes=[
             pltpu.VMEM((2, 2 * HALO, nz // LANES, wide, LANES), jnp.float32),
             pltpu.VMEM((2, 32, nz), jnp.float32),
-            big,
-            big,
+            pltpu.VMEM((2, tall, wide, nz), jnp.float32),
             big,
             big,
             pltpu.VMEM((nx, nz // LANES, wide, LANES), jnp.float32),

time: 122 us -> 139 us (1.14); the launches traced: 121 us -> 140 us
  Pallas kernels: 57.4 us -> 71.2 us
  starting transfers between devices: 48.2 us -> 52.9 us
    pallas_call x1, Pallas kernels: 21 us -> 38.1 us  [heat(): pl.pallas_call(heat_kernel, out_shape=(jax.ShapeDtypeStruct(shape, jnp.fl...]
    all_to_all x5, starting transfers between devices: 31.8 us -> 36.5 us  [exchange(): lax.all_to_all(rows, ('slab', 'pair'), split_axis=0, concat_axis=0, tiled...]
    pallas_call x2, Pallas kernels: 15.5 us -> 12.2 us  [tile_terms(): pl.pallas_call(tiles_kernel, out_shape=jax.ShapeDtypeStruct(whole.shape,...]
    ppermute x3, waiting for transfers between devices: 1.35 us -> 2.9 us  [both_ways(): from_high = lax.ppermute(low, axis, backward)]
  transfers between devices with their start and end apart: 11 -> 11, of which waited for: 7 -> 6; matrix products, arithmetic and copies ran while one was open for 2% -> 2% of each run, Pallas kernels for 40% -> 45%
where the time goes in v3:
time: 139 us; the launch traced here: 140 us
  Pallas kernels  71.2 us (51%)
  starting transfers between devices  52.9 us (38%)
  waiting for transfers between devices  12.1 us (9%)
  local copies, waits for them, and re-layouts  2.25 us (2%)
  between operations  1.42 us (1%)
    pallas_call x1, Pallas kernels, heat(): pl.pallas_call(heat_kernel, out_shape=(jax.ShapeDtypeStruct(shape, jnp.fl...  38.1 us
    all_to_all x5, starting transfers between devices, exchange(): lax.all_to_all(rows, ('slab', 'pair'), split_axis=0, concat_axis=0, tiled...  36.5 us
    ppermute x3, starting transfers between devices, both_ways(): from_low = lax.ppermute(high, axis, forward)  12.6 us
    pallas_call x2, Pallas kernels, tile_terms(): pl.pallas_call(tiles_kernel, out_shape=jax.ShapeDtypeStruct(whole.shape,...  12.2 us
    pallas_call x1, Pallas kernels, own_planes(): pl.pallas_call(own_planes_kernel, out_shape=(shape, shape, shape, jax.Sha...  7.93 us
    all_to_all x5, waiting for transfers between devices, exchange(): lax.all_to_all(rows, ('slab', 'pair'), split_axis=0, concat_axis=0, tiled...  5.25 us
    ppermute x3, waiting for transfers between devices, both_ways(): from_low = lax.ppermute(high, axis, forward)  3.92 us
    ppermute x3, starting transfers between devices, both_ways(): from_high = lax.ppermute(low, axis, backward)  3.84 us
  transfers between devices with their start and end apart: 11, of which 6 were waited for; matrix products, arithmetic and copies ran while one was open for 2% of the time, Pallas kernels for 45%

profile of v3, /device:TPU:0, one launch (start us, length us, event | category | flops | bytes accessed | tf_op | source)
XLA Modules:
  0.0 139.8 jit_solution(1029988816498126732)
XLA Ops:
  0.6 2.1 %emit.1 = (f32[16,128]{1,0:T(8,128)}, f32[32,16,128]{2,1,0:T(8,128)}) custom-call(f32[16,64,512]{2,1,0:T(8,128)} %t_ref, s32[16,128]{1,0:T(8,128)} %site_ref.3, f32[16,128]{1,0:T(8,128)} %mirror_ref.5), custom_call_target="tpu_custom_call" | custom-call | flops 10000 | bytes 900000 | tf_op jit(solution)/shard_map/emit/pallas_call | solution.py:96
  2.8 7.4 %all-to-all-start = ((f32[32,16,128]{2,1,0:T(8,128)}), f32[32,16,128]{2,1,0:T(8,128)}, u32[]{:S(2)}, u32[]{:S(2)}) async-start(f32[32,16,128]{2,1,0:T(8,128)} %get-tuple-element.48), calls=%async_computation | async-start | bytes 524288 | tf_op jit(solution)/shard_map/all_to_all | solution.py:829
  10.2 2.3 %fusion = (f32[4,64,512]{2,1,0:T(8,128)}, f32[4,64,512]{2,1,0:T(8,128)}) fusion(f32[16,64,512]{2,1,0:T(8,128)} %k_ref), kind=kLoop, calls=%fused_computation | loop fusion | bytes 2097152 | tf_op jit(solution)/shard_map/slice | solution.py:871
  12.5 4.4 %collective-permute-start.2 = (f32[4,64,512]{2,1,0:T(8,128)}, f32[4,64,512]{2,1,0:T(8,128)}, u32[]{:S(2)}, u32[]{:S(2)}) collective-permute-start(f32[4,64,512]{2,1,0:T(8,128)} %get-tuple-element.90), channel_id=1, source_target_pairs={{0,4},{4,8},{8,12},{12,16},{16,20},{20,24},{24,28},{1,5},{5,9},{9,... | collective-permute-start | bytes 1572872 | tf_op jit(solution)/shard_map/ppermute | solution.py:840
  16.9 1.3 collective-permute-start.3
  18.8 2.0 %all-to-all-done = f32[32,16,128]{2,1,0:T(8,128)} async-done(((f32[32,16,128]{2,1,0:T(8,128)}), f32[32,16,128]{2,1,0:T(8,128)}, u32[]{:S(2)}, u32[]{:S(2)}) %all-to-all-start) | async-done | bytes 262176 | tf_op jit(solution)/shard_map/all_to_all | solution.py:829
  20.8 6.1 %tiles.2 = f32[512,128]{1,0:T(8,128)} custom-call(s32[1]{0:T(128)S(6)} %copy.11.live_ref, s32[2,256]{1,0:T(2,128)} %bitcast.7, s32[2,256]{1,0:T(2,128)} %bitcast.8, f32[512,128]{1,0:T(8,128)} %bitcast.1.whole_ref, f32[256,128,128]{2,1,0:T(8,128)} %tiles_ref.3), custom_call_target="tpu_custom_call" | custom-call | flops 134217728 | bytes 16777216 | tf_op jit(solution)/shard_map/tiles/pallas_call | solution.py:200
  26.9 9.1 %all-to-all-start.1 = ((f32[32,16,128]{2,1,0:T(8,128)}), f32[32,16,128]{2,1,0:T(8,128)}, u32[]{:S(2)}, u32[]{:S(2)}) async-start(f32[32,16,128]{2,1,0:T(8,128)} %bitcast.5), calls=%async_computation.1 | async-start | bytes 524288 | tf_op jit(solution)/shard_map/all_to_all | solution.py:829
  36.0 2.0 %pack_y.1 = (f32[16,8,512]{2,1,0:T(8,128)}, f32[16,8,512]{2,1,0:T(8,128)}) custom-call(f32[16,64,512]{2,1,0:T(8,128)} %t_ref, f32[16,64,512]{2,1,0:T(8,128)} %k_ref, f32[16,64,512]{2,1,0:T(8,128)} %t_ref, f32[16,64,512]{2,1,0:T(8,128)} %k_ref), custom_call_target="tpu_custom_call" | custom-call | bytes 1048576 | tf_op jit(solution)/shard_map/pack_y/pallas_call | solution.py:297
  38.1 2.8 %collective-permute-start = (f32[16,8,512]{2,1,0:T(8,128)}, f32[16,8,512]{2,1,0:T(8,128)}, u32[]{:S(2)}, u32[]{:S(2)}) collective-permute-start(f32[16,8,512]{2,1,0:T(8,128)} %get-tuple-element.54), channel_id=1, source_target_pairs={{0,1},{1,2},{2,3},{4,5},{5,6},{6,7},{8,9},{9,10},{10,11},{12,13},{... | collective-permute-start | bytes 786440 | tf_op jit(solution)/shard_map/ppermute | solution.py:840
  40.8 1.3 collective-permute-start.1
  42.1 0.0 collective-permute-done.2.k_low
  42.1 0.0 collective-permute-done.3.k_high
  42.1 0.0 collective-permute-done.below0.below1.below_ref
  42.1 2.9 %collective-permute-done.1.above0.above1.above_ref = f32[16,8,512]{2,1,0:T(8,128)} collective-permute-done((f32[16,8,512]{2,1,0:T(8,128)}, f32[16,8,512]{2,1,0:T(8,128)}, u32[]{:S(2)}, u32[]{:S(2)}) %collective-permute-start.1) | collective-permute-done | bytes 262176 | tf_op jit(solution)/shard_map/ppermute | solution.py:841
  45.0 1.5 %all-to-all-done.1.parts_ref = f32[32,16,128]{2,1,0:T(8,128)} async-done(((f32[32,16,128]{2,1,0:T(8,128)}), f32[32,16,128]{2,1,0:T(8,128)}, u32[]{:S(2)}, u32[]{:S(2)}) %all-to-all-start.1) | async-done | bytes 262176 | tf_op jit(solution)/shard_map/all_to_all | solution.py:829
  46.6 1.7 %middle.1 = f32[32,16,128]{2,1,0:T(8,128)} custom-call(f32[32,16,128]{2,1,0:T(8,128)} %all-to-all-done.1.parts_ref, f32[16,128]{1,0:T(8,128)} %get-tuple-element.57.emitted_ref, f32[16,128]{1,0:T(8,128)} %mirror_ref.5), custom_call_target="tpu_custom_call" | custom-call | flops 100000 | bytes 600000 | tf_op jit(solution)/shard_map/middle/pallas_call | solution.py:233
  48.3 7.6 %all-to-all-start.2 = ((f32[32,16,128]{2,1,0:T(8,128)}), f32[32,16,128]{2,1,0:T(8,128)}, u32[]{:S(2)}, u32[]{:S(2)}) async-start(f32[32,16,128]{2,1,0:T(8,128)} %middle.1), calls=%async_computation.2 | async-start | bytes 524288 | tf_op jit(solution)/shard_map/all_to_all | solution.py:829
  55.9 2.3 %pack_x.1 = (f32[288,512]{1,0:T(8,128)}, f32[288,512]{1,0:T(8,128)}) custom-call(f32[16,64,512]{2,1,0:T(8,128)} %t_ref, f32[16,64,512]{2,1,0:T(8,128)} %t_ref, f32[16,8,512]{2,1,0:T(8,128)} %collective-permute-done.below0.below1.below_ref, f32[16,8,512]{2,1,0:T(8,128)} %collective-permute-done.1.above0.above1.above_ref, ...), custom_call_target="tpu_custom_call" | custom-call | bytes 2359296 | tf_op jit(solution)/shard_map/pack_x/pallas_call | solution.py:357
  58.2 1.3 collective-permute-start.5
  59.5 5.4 %collective-permute-start.4 = (f32[288,512]{1,0:T(8,128)}, f32[288,512]{1,0:T(8,128)}, u32[]{:S(2)}, u32[]{:S(2)}) collective-permute-start(f32[288,512]{1,0:T(8,128)} %get-tuple-element.64), channel_id=1, source_target_pairs={{0,4},{4,8},{8,12},{12,16},{16,20},{20,24},{24,28},{1,5},{5,9},{9,... | collective-permute-start | bytes 1769480 | tf_op jit(solution)/shard_map/ppermute | solution.py:840
  64.9 1.6 %all-to-all-done.2 = f32[32,16,128]{2,1,0:T(8,128)} async-done(((f32[32,16,128]{2,1,0:T(8,128)}), f32[32,16,128]{2,1,0:T(8,128)}, u32[]{:S(2)}, u32[]{:S(2)}) %all-to-all-start.2) | async-done | bytes 262176 | tf_op jit(solution)/shard_map/all_to_all | solution.py:829
  66.4 6.1 %tiles.3 = f32[512,128]{1,0:T(8,128)} custom-call(s32[1]{0:T(128)S(6)} %copy.11.live_ref, s32[2,256]{1,0:T(2,128)} %bitcast.9, s32[2,256]{1,0:T(2,128)} %bitcast.10, f32[512,128]{1,0:T(8,128)} %bitcast.3.whole_ref, f32[256,128,128]{2,1,0:T(8,128)} %tiles_ref.3), custom_call_target="tpu_custom_call" | custom-call | flops 134217728 | bytes 16777216 | tf_op jit(solution)/shard_map/tiles/pallas_call | solution.py:200
  72.6 7.3 %all-to-all-start.3 = ((f32[32,16,128]{2,1,0:T(8,128)}), f32[32,16,128]{2,1,0:T(8,128)}, u32[]{:S(2)}, u32[]{:S(2)}) async-start(f32[32,16,128]{2,1,0:T(8,128)} %bitcast.6), calls=%async_computation.3 | async-start | bytes 524288 | tf_op jit(solution)/shard_map/all_to_all | solution.py:829
  79.9 7.9 %own_planes.1 = (f32[16,72,512]{2,1,0:T(8,128)}, f32[16,72,512]{2,1,0:T(8,128)}, f32[16,72,512]{2,1,0:T(8,128)}, f32[16,8,128]{2,1,0:T(8,128)}) custom-call(f32[16,64,512]{2,1,0:T(8,128)} %t_ref, f32[16,64,512]{2,1,0:T(8,128)} %k_ref, f32[16,8,512]{2,1,0:T(8,128)} %collective-permute-done.below0.below1.below_ref, ...), custom_call_target="tpu_custom_call" | custom-call | flops 5898240 | bytes 14155776 | tf_op jit(solution)/shard_map/own_planes/pallas_call | solution.py:579
  87.8 0.0 collective-permute-done.5.t_high
  87.8 3.9 %collective-permute-done.4.t_low = f32[288,512]{1,0:T(8,128)} collective-permute-done((f32[288,512]{1,0:T(8,128)}, f32[288,512]{1,0:T(8,128)}, u32[]{:S(2)}, u32[]{:S(2)}) %collective-permute-start.4) | collective-permute-done | bytes 589856 | tf_op jit(solution)/shard_map/ppermute | solution.py:840
  91.8 0.2 all-to-all-done.3.parts_ref
  91.9 2.2 %last.1 = (f32[16,128]{1,0:T(8,128)}, f32[32,8,128]{2,1,0:T(8,128)}) custom-call(f32[32,16,128]{2,1,0:T(8,128)} %all-to-all-done.3.parts_ref, f32[16,128]{1,0:T(8,128)} %get-tuple-element.57.emitted_ref, f32[16,128]{1,0:T(8,128)} %mirror_ref.5, s32[16,128]{1,0:T(8,128)} %site_ref.3), custom_call_target="tpu_custom_call" | custom-call | flops 10000000 | bytes 600000 | tf_op jit(solution)/shard_map/last/pallas_call | solution.py:273
  94.1 5.1 %all-to-all-start.4 = ((f32[32,8,128]{2,1,0:T(8,128)}), f32[32,8,128]{2,1,0:T(8,128)}, u32[]{:S(2)}, u32[]{:S(2)}) async-start(f32[32,8,128]{2,1,0:T(8,128)} %get-tuple-element.75), calls=%async_computation.4 | async-start | bytes 262144 | tf_op jit(solution)/shard_map/all_to_all | solution.py:829
  99.2 38.1 %heat.1 = (f32[16,64,512]{2,1,0:T(8,128)}, f32[24,8,128]{2,1,0:T(8,128)}) custom-call(f32[16,72,512]{2,1,0:T(8,128)} %get-tuple-element.80.own_field, f32[16,72,512]{2,1,0:T(8,128)} %get-tuple-element.81.own_faces, f32[16,72,512]{2,1,0:T(8,128)} %get-tuple-element.82.own_gz, f32[16,8,128]{2,1,0:T(8,128)} %get-tuple-element.83.own_thin, ...), custom_call_target="tpu_custom_call" | custom-call | flops 88473600 | bytes 25165824 | tf_op jit(solution)/shard_map/heat/pallas_call | solution.py:703
  137.2 0.0 all-to-all-done.4.all_ref
  137.2 2.6 %add_source.1 = f32[16,64,512]{2,1,0:T(8,128)} custom-call(f32[32,8,128]{2,1,0:T(8,128)} %all-to-all-done.4.all_ref, f32[24,8,128]{2,1,0:T(8,128)} %get-tuple-element.88.thin_ref, f32[16,64,512]{2,1,0:T(8,128)} %get-tuple-element.89.base_ref), custom_call_target="tpu_custom_call", output_to_operand_aliasing={{}: (2, {})} | custom-call | flops 1000000 | bytes 1048576 | tf_op jit(solution)/shard_map/add_source/pallas_call | solution.py:811
Async XLA Ops:
  2.8 18.0 %all-to-all-start = ((f32[32,16,128]{2,1,0:T(8,128)}), f32[32,16,128]{2,1,0:T(8,128)}, u32[]{:S(2)}, u32[]{:S(2)}) async-start(f32[32,16,128]{2,1,0:T(8,128)} %get-tuple-element.48), calls=%async_computation | async-start | bytes 524288 | tf_op jit(solution)/shard_map/all_to_all | solution.py:829
  12.5 29.7 %collective-permute-start.2 = (f32[4,64,512]{2,1,0:T(8,128)}, f32[4,64,512]{2,1,0:T(8,128)}, u32[]{:S(2)}, u32[]{:S(2)}) collective-permute-start(f32[4,64,512]{2,1,0:T(8,128)} %get-tuple-element.90), channel_id=1, source_target_pairs={{0,4},{4,8},{8,12},{12,16},{16,20},{20,24},{24,28},{1,5},{5,9},{9,... | collective-permute-start | bytes 1572872 | tf_op jit(solution)/shard_map/ppermute | solution.py:840
  16.9 25.3 %collective-permute-start.3 = (f32[4,64,512]{2,1,0:T(8,128)}, f32[4,64,512]{2,1,0:T(8,128)}, u32[]{:S(2)}, u32[]{:S(2)}) collective-permute-start(f32[4,64,512]{2,1,0:T(8,128)} %get-tuple-element.91), channel_id=1, source_target_pairs={{4,0},{8,4},{12,8},{16,12},{20,16},{24,20},{28,24},{5,1},{9,5},{13... | collective-permute-start | bytes 1572872 | tf_op jit(solution)/shard_map/ppermute | solution.py:841
  26.9 19.7 %all-to-all-start.1 = ((f32[32,16,128]{2,1,0:T(8,128)}), f32[32,16,128]{2,1,0:T(8,128)}, u32[]{:S(2)}, u32[]{:S(2)}) async-start(f32[32,16,128]{2,1,0:T(8,128)} %bitcast.5), calls=%async_computation.1 | async-start | bytes 524288 | tf_op jit(solution)/shard_map/all_to_all | solution.py:829
  38.1 4.1 %collective-permute-start = (f32[16,8,512]{2,1,0:T(8,128)}, f32[16,8,512]{2,1,0:T(8,128)}, u32[]{:S(2)}, u32[]{:S(2)}) collective-permute-start(f32[16,8,512]{2,1,0:T(8,128)} %get-tuple-element.54), channel_id=1, source_target_pairs={{0,1},{1,2},{2,3},{4,5},{5,6},{6,7},{8,9},{9,10},{10,11},{12,13},{... | collective-permute-start | bytes 786440 | tf_op jit(solution)/shard_map/ppermute | solution.py:840
  40.8 4.2 %collective-permute-start.1 = (f32[16,8,512]{2,1,0:T(8,128)}, f32[16,8,512]{2,1,0:T(8,128)}, u32[]{:S(2)}, u32[]{:S(2)}) collective-permute-start(f32[16,8,512]{2,1,0:T(8,128)} %get-tuple-element.55), channel_id=1, source_target_pairs={{1,0},{2,1},{3,2},{5,4},{6,5},{7,6},{9,8},{10,9},{11,10},{13,12},{... | collective-permute-start | bytes 786440 | tf_op jit(solution)/shard_map/ppermute | solution.py:841
  48.3 18.1 %all-to-all-start.2 = ((f32[32,16,128]{2,1,0:T(8,128)}), f32[32,16,128]{2,1,0:T(8,128)}, u32[]{:S(2)}, u32[]{:S(2)}) async-start(f32[32,16,128]{2,1,0:T(8,128)} %middle.1), calls=%async_computation.2 | async-start | bytes 524288 | tf_op jit(solution)/shard_map/all_to_all | solution.py:829
  58.2 29.6 %collective-permute-start.5 = (f32[288,512]{1,0:T(8,128)}, f32[288,512]{1,0:T(8,128)}, u32[]{:S(2)}, u32[]{:S(2)}) collective-permute-start(f32[288,512]{1,0:T(8,128)} %get-tuple-element.63), channel_id=1, source_target_pairs={{4,0},{8,4},{12,8},{16,12},{20,16},{24,20},{28,24},{5,1},{9,5},{13... | collective-permute-start | bytes 1769480 | tf_op jit(solution)/shard_map/ppermute | solution.py:841
  59.5 32.3 %collective-permute-start.4 = (f32[288,512]{1,0:T(8,128)}, f32[288,512]{1,0:T(8,128)}, u32[]{:S(2)}, u32[]{:S(2)}) collective-permute-start(f32[288,512]{1,0:T(8,128)} %get-tuple-element.64), channel_id=1, source_target_pairs={{0,4},{4,8},{8,12},{12,16},{16,20},{20,24},{24,28},{1,5},{5,9},{9,... | collective-permute-start | bytes 1769480 | tf_op jit(solution)/shard_map/ppermute | solution.py:840
  72.6 19.4 %all-to-all-start.3 = ((f32[32,16,128]{2,1,0:T(8,128)}), f32[32,16,128]{2,1,0:T(8,128)}, u32[]{:S(2)}, u32[]{:S(2)}) async-start(f32[32,16,128]{2,1,0:T(8,128)} %bitcast.6), calls=%async_computation.3 | async-start | bytes 524288 | tf_op jit(solution)/shard_map/all_to_all | solution.py:829
  94.1 43.1 %all-to-all-start.4 = ((f32[32,8,128]{2,1,0:T(8,128)}), f32[32,8,128]{2,1,0:T(8,128)}, u32[]{:S(2)}, u32[]{:S(2)}) async-start(f32[32,8,128]{2,1,0:T(8,128)} %get-tuple-element.75), calls=%async_computation.4 | async-start | bytes 262144 | tf_op jit(solution)/shard_map/all_to_all | solution.py:829

commit v4 on v1

--- a/solution.py
+++ b/solution.py
@@ -14,7 +14,7 @@
 ROWS = STEPS
 LANES = 128
 CHUNK = 16
-LAG = 8
+LAG = 0
 
 step_size = 0.07
 

time: 122 us -> 123 us (level)
  starting transfers between devices: 48.2 us -> 50.9 us
    all_to_all x5, starting transfers between devices: 31.8 us -> 34.5 us  [exchange(): lax.all_to_all(rows, ('slab', 'pair'), split_axis=0, concat_axis=0, tiled...]
    ppermute x3, waiting for transfers between devices: 1.35 us -> 2.9 us  [both_ways(): from_high = lax.ppermute(low, axis, backward)]
    ppermute x3, waiting for transfers between devices: 5.16 us -> 3.67 us  [both_ways(): from_low = lax.ppermute(high, axis, forward)]
  transfers between devices with their start and end apart: 11 -> 11, of which waited for: 7 -> 6; matrix products, arithmetic and copies ran while one was open for 2% -> 2% of each run, Pallas kernels for 40% -> 39%
where the time goes in v4:
time: 123 us
  Pallas kernels  56.4 us (46%)
  starting transfers between devices  50.9 us (41%)
  waiting for transfers between devices  11.8 us (10%)
  local copies, waits for them, and re-layouts  2.25 us (2%)
  between operations  1.42 us (1%)
    all_to_all x5, starting transfers between devices, exchange(): lax.all_to_all(rows, ('slab', 'pair'), split_axis=0, concat_axis=0, tiled...  34.5 us
    pallas_call x1, Pallas kernels, heat(): pl.pallas_call(heat_kernel, out_shape=(jax.ShapeDtypeStruct(shape, jnp.fl...  21 us
    pallas_call x2, Pallas kernels, tile_terms(): pl.pallas_call(tiles_kernel, out_shape=jax.ShapeDtypeStruct(whole.shape,...  14.4 us
    ppermute x3, starting transfers between devices, both_ways(): from_low = lax.ppermute(high, axis, forward)  12.6 us
    pallas_call x1, Pallas kernels, own_planes(): pl.pallas_call(own_planes_kernel, out_shape=(shape, shape, shape, jax.Sha...  7.93 us
    all_to_all x5, waiting for transfers between devices, exchange(): lax.all_to_all(rows, ('slab', 'pair'), split_axis=0, concat_axis=0, tiled...  5.25 us
    ppermute x3, starting transfers between devices, both_ways(): from_high = lax.ppermute(low, axis, backward)  3.84 us
    ppermute x3, waiting for transfers between devices, both_ways(): from_low = lax.ppermute(high, axis, forward)  3.67 us
  transfers between devices with their start and end apart: 11, of which 6 were waited for; matrix products, arithmetic and copies ran while one was open for 2% of the time, Pallas kernels for 39%

profile of v4, /device:TPU:0, one launch (start us, length us, event | category | flops | bytes accessed | tf_op | source)
XLA Modules:
  0.0 122.7 jit_solution(7243083290541012219)
XLA Ops:
  0.6 2.1 %emit.1 = (f32[16,128]{1,0:T(8,128)}, f32[32,16,128]{2,1,0:T(8,128)}) custom-call(f32[16,64,512]{2,1,0:T(8,128)} %t_ref, s32[16,128]{1,0:T(8,128)} %site_ref.3, f32[16,128]{1,0:T(8,128)} %mirror_ref.5), custom_call_target="tpu_custom_call" | custom-call | flops 10000 | bytes 900000 | tf_op jit(solution)/shard_map/emit/pallas_call | solution.py:96
  2.8 7.4 %all-to-all-start = ((f32[32,16,128]{2,1,0:T(8,128)}), f32[32,16,128]{2,1,0:T(8,128)}, u32[]{:S(2)}, u32[]{:S(2)}) async-start(f32[32,16,128]{2,1,0:T(8,128)} %get-tuple-element.48), calls=%async_computation | async-start | bytes 524288 | tf_op jit(solution)/shard_map/all_to_all | solution.py:827
  10.2 2.3 %fusion = (f32[4,64,512]{2,1,0:T(8,128)}, f32[4,64,512]{2,1,0:T(8,128)}) fusion(f32[16,64,512]{2,1,0:T(8,128)} %k_ref), kind=kLoop, calls=%fused_computation | loop fusion | bytes 2097152 | tf_op jit(solution)/shard_map/slice | solution.py:869
  12.5 4.4 %collective-permute-start.2 = (f32[4,64,512]{2,1,0:T(8,128)}, f32[4,64,512]{2,1,0:T(8,128)}, u32[]{:S(2)}, u32[]{:S(2)}) collective-permute-start(f32[4,64,512]{2,1,0:T(8,128)} %get-tuple-element.90), channel_id=1, source_target_pairs={{0,4},{4,8},{8,12},{12,16},{16,20},{20,24},{24,28},{1,5},{5,9},{9,... | collective-permute-start | bytes 1572872 | tf_op jit(solution)/shard_map/ppermute | solution.py:838
  16.9 1.3 %collective-permute-start.3 = (f32[4,64,512]{2,1,0:T(8,128)}, f32[4,64,512]{2,1,0:T(8,128)}, u32[]{:S(2)}, u32[]{:S(2)}) collective-permute-start(f32[4,64,512]{2,1,0:T(8,128)} %get-tuple-element.91), channel_id=1, source_target_pairs={{4,0},{8,4},{12,8},{16,12},{20,16},{24,20},{28,24},{5,1},{9,5},{13... | collective-permute-start | bytes 1572872 | tf_op jit(solution)/shard_map/ppermute | solution.py:839
  18.8 2.0 %all-to-all-done = f32[32,16,128]{2,1,0:T(8,128)} async-done(((f32[32,16,128]{2,1,0:T(8,128)}), f32[32,16,128]{2,1,0:T(8,128)}, u32[]{:S(2)}, u32[]{:S(2)}) %all-to-all-start) | async-done | bytes 262176 | tf_op jit(solution)/shard_map/all_to_all | solution.py:827
  20.8 7.2 %tiles.2 = f32[512,128]{1,0:T(8,128)} custom-call(s32[1]{0:T(128)S(6)} %copy.11.live_ref, s32[2,256]{1,0:T(2,128)} %bitcast.7, s32[2,256]{1,0:T(2,128)} %bitcast.8, f32[512,128]{1,0:T(8,128)} %bitcast.1.whole_ref, f32[256,128,128]{2,1,0:T(8,128)} %tiles_ref.3), custom_call_target="tpu_custom_call" | custom-call | flops 134217728 | bytes 16777216 | tf_op jit(solution)/shard_map/tiles/pallas_call | solution.py:200
  28.0 8.0 %all-to-all-start.1 = ((f32[32,16,128]{2,1,0:T(8,128)}), f32[32,16,128]{2,1,0:T(8,128)}, u32[]{:S(2)}, u32[]{:S(2)}) async-start(f32[32,16,128]{2,1,0:T(8,128)} %bitcast.5), calls=%async_computation.1 | async-start | bytes 524288 | tf_op jit(solution)/shard_map/all_to_all | solution.py:827
  35.9 2.0 %pack_y.1 = (f32[16,8,512]{2,1,0:T(8,128)}, f32[16,8,512]{2,1,0:T(8,128)}) custom-call(f32[16,64,512]{2,1,0:T(8,128)} %t_ref, f32[16,64,512]{2,1,0:T(8,128)} %k_ref, f32[16,64,512]{2,1,0:T(8,128)} %t_ref, f32[16,64,512]{2,1,0:T(8,128)} %k_ref), custom_call_target="tpu_custom_call" | custom-call | bytes 1048576 | tf_op jit(solution)/shard_map/pack_y/pallas_call | solution.py:297
  38.0 2.8 %collective-permute-start = (f32[16,8,512]{2,1,0:T(8,128)}, f32[16,8,512]{2,1,0:T(8,128)}, u32[]{:S(2)}, u32[]{:S(2)}) collective-permute-start(f32[16,8,512]{2,1,0:T(8,128)} %get-tuple-element.54), channel_id=1, source_target_pairs={{0,1},{1,2},{2,3},{4,5},{5,6},{6,7},{8,9},{9,10},{10,11},{12,13},{... | collective-permute-start | bytes 786440 | tf_op jit(solution)/shard_map/ppermute | solution.py:838
  40.7 1.3 %collective-permute-start.1 = (f32[16,8,512]{2,1,0:T(8,128)}, f32[16,8,512]{2,1,0:T(8,128)}, u32[]{:S(2)}, u32[]{:S(2)}) collective-permute-start(f32[16,8,512]{2,1,0:T(8,128)} %get-tuple-element.55), channel_id=1, source_target_pairs={{1,0},{2,1},{3,2},{5,4},{6,5},{7,6},{9,8},{10,9},{11,10},{13,12},{... | collective-permute-start | bytes 786440 | tf_op jit(solution)/shard_map/ppermute | solution.py:839
  42.0 0.0 collective-permute-done.2.k_low
  42.0 0.0 collective-permute-done.3.k_high
  42.1 0.0 collective-permute-done.below0.below1.below_ref
  42.1 2.9 %collective-permute-done.1.above0.above1.above_ref = f32[16,8,512]{2,1,0:T(8,128)} collective-permute-done((f32[16,8,512]{2,1,0:T(8,128)}, f32[16,8,512]{2,1,0:T(8,128)}, u32[]{:S(2)}, u32[]{:S(2)}) %collective-permute-start.1) | collective-permute-done | bytes 262176 | tf_op jit(solution)/shard_map/ppermute | solution.py:839
  45.0 1.5 %all-to-all-done.1.parts_ref = f32[32,16,128]{2,1,0:T(8,128)} async-done(((f32[32,16,128]{2,1,0:T(8,128)}), f32[32,16,128]{2,1,0:T(8,128)}, u32[]{:S(2)}, u32[]{:S(2)}) %all-to-all-start.1) | async-done | bytes 262176 | tf_op jit(solution)/shard_map/all_to_all | solution.py:827
  46.5 1.7 %middle.1 = f32[32,16,128]{2,1,0:T(8,128)} custom-call(f32[32,16,128]{2,1,0:T(8,128)} %all-to-all-done.1.parts_ref, f32[16,128]{1,0:T(8,128)} %get-tuple-element.57.emitted_ref, f32[16,128]{1,0:T(8,128)} %mirror_ref.5), custom_call_target="tpu_custom_call" | custom-call | flops 100000 | bytes 600000 | tf_op jit(solution)/shard_map/middle/pallas_call | solution.py:233
  48.2 7.6 %all-to-all-start.2 = ((f32[32,16,128]{2,1,0:T(8,128)}), f32[32,16,128]{2,1,0:T(8,128)}, u32[]{:S(2)}, u32[]{:S(2)}) async-start(f32[32,16,128]{2,1,0:T(8,128)} %middle.1), calls=%async_computation.2 | async-start | bytes 524288 | tf_op jit(solution)/shard_map/all_to_all | solution.py:827
  55.8 2.3 %pack_x.1 = (f32[288,512]{1,0:T(8,128)}, f32[288,512]{1,0:T(8,128)}) custom-call(f32[16,64,512]{2,1,0:T(8,128)} %t_ref, f32[16,64,512]{2,1,0:T(8,128)} %t_ref, f32[16,8,512]{2,1,0:T(8,128)} %collective-permute-done.below0.below1.below_ref, f32[16,8,512]{2,1,0:T(8,128)} %collective-permute-done.1.above0.above1.above_ref, ...), custom_call_target="tpu_custom_call" | custom-call | bytes 2359296 | tf_op jit(solution)/shard_map/pack_x/pallas_call | solution.py:357
  58.1 1.3 %collective-permute-start.5 = (f32[288,512]{1,0:T(8,128)}, f32[288,512]{1,0:T(8,128)}, u32[]{:S(2)}, u32[]{:S(2)}) collective-permute-start(f32[288,512]{1,0:T(8,128)} %get-tuple-element.63), channel_id=1, source_target_pairs={{4,0},{8,4},{12,8},{16,12},{20,16},{24,20},{28,24},{5,1},{9,5},{13... | collective-permute-start | bytes 1769480 | tf_op jit(solution)/shard_map/ppermute | solution.py:839
  59.4 5.4 %collective-permute-start.4 = (f32[288,512]{1,0:T(8,128)}, f32[288,512]{1,0:T(8,128)}, u32[]{:S(2)}, u32[]{:S(2)}) collective-permute-start(f32[288,512]{1,0:T(8,128)} %get-tuple-element.64), channel_id=1, source_target_pairs={{0,4},{4,8},{8,12},{12,16},{16,20},{20,24},{24,28},{1,5},{5,9},{9,... | collective-permute-start | bytes 1769480 | tf_op jit(solution)/shard_map/ppermute | solution.py:838
  64.8 1.6 %all-to-all-done.2 = f32[32,16,128]{2,1,0:T(8,128)} async-done(((f32[32,16,128]{2,1,0:T(8,128)}), f32[32,16,128]{2,1,0:T(8,128)}, u32[]{:S(2)}, u32[]{:S(2)}) %all-to-all-start.2) | async-done | bytes 262176 | tf_op jit(solution)/shard_map/all_to_all | solution.py:827
  66.4 7.2 %tiles.3 = f32[512,128]{1,0:T(8,128)} custom-call(s32[1]{0:T(128)S(6)} %copy.11.live_ref, s32[2,256]{1,0:T(2,128)} %bitcast.9, s32[2,256]{1,0:T(2,128)} %bitcast.10, f32[512,128]{1,0:T(8,128)} %bitcast.3.whole_ref, f32[256,128,128]{2,1,0:T(8,128)} %tiles_ref.3), custom_call_target="tpu_custom_call" | custom-call | flops 134217728 | bytes 16777216 | tf_op jit(solution)/shard_map/tiles/pallas_call | solution.py:200
  73.6 6.5 %all-to-all-start.3 = ((f32[32,16,128]{2,1,0:T(8,128)}), f32[32,16,128]{2,1,0:T(8,128)}, u32[]{:S(2)}, u32[]{:S(2)}) async-start(f32[32,16,128]{2,1,0:T(8,128)} %bitcast.6), calls=%async_computation.3 | async-start | bytes 524288 | tf_op jit(solution)/shard_map/all_to_all | solution.py:827
  80.1 7.9 %own_planes.1 = (f32[16,72,512]{2,1,0:T(8,128)}, f32[16,72,512]{2,1,0:T(8,128)}, f32[16,72,512]{2,1,0:T(8,128)}, f32[16,8,128]{2,1,0:T(8,128)}) custom-call(f32[16,64,512]{2,1,0:T(8,128)} %t_ref, f32[16,64,512]{2,1,0:T(8,128)} %k_ref, f32[16,8,512]{2,1,0:T(8,128)} %collective-permute-done.below0.below1.below_ref, ...), custom_call_target="tpu_custom_call" | custom-call | flops 5898240 | bytes 14155776 | tf_op jit(solution)/shard_map/own_planes/pallas_call | solution.py:579
  88.0 0.0 collective-permute-done.5.t_high
  88.0 3.7 %collective-permute-done.4.t_low = f32[288,512]{1,0:T(8,128)} collective-permute-done((f32[288,512]{1,0:T(8,128)}, f32[288,512]{1,0:T(8,128)}, u32[]{:S(2)}, u32[]{:S(2)}) %collective-permute-start.4) | collective-permute-done | bytes 589856 | tf_op jit(solution)/shard_map/ppermute | solution.py:838
  91.7 0.2 all-to-all-done.3.parts_ref
  91.8 2.2 %last.1 = (f32[16,128]{1,0:T(8,128)}, f32[32,8,128]{2,1,0:T(8,128)}) custom-call(f32[32,16,128]{2,1,0:T(8,128)} %all-to-all-done.3.parts_ref, f32[16,128]{1,0:T(8,128)} %get-tuple-element.57.emitted_ref, f32[16,128]{1,0:T(8,128)} %mirror_ref.5, s32[16,128]{1,0:T(8,128)} %site_ref.3), custom_call_target="tpu_custom_call" | custom-call | flops 10000000 | bytes 600000 | tf_op jit(solution)/shard_map/last/pallas_call | solution.py:273
  94.0 5.1 %all-to-all-start.4 = ((f32[32,8,128]{2,1,0:T(8,128)}), f32[32,8,128]{2,1,0:T(8,128)}, u32[]{:S(2)}, u32[]{:S(2)}) async-start(f32[32,8,128]{2,1,0:T(8,128)} %get-tuple-element.75), calls=%async_computation.4 | async-start | bytes 262144 | tf_op jit(solution)/shard_map/all_to_all | solution.py:827
  99.1 21.0 %heat.1 = (f32[16,64,512]{2,1,0:T(8,128)}, f32[24,8,128]{2,1,0:T(8,128)}) custom-call(f32[16,72,512]{2,1,0:T(8,128)} %get-tuple-element.80.own_field, f32[16,72,512]{2,1,0:T(8,128)} %get-tuple-element.81.own_faces, f32[16,72,512]{2,1,0:T(8,128)} %get-tuple-element.82.own_gz, f32[16,8,128]{2,1,0:T(8,128)} %get-tuple-element.83.own_thin, ...), custom_call_target="tpu_custom_call" | custom-call | flops 88473600 | bytes 25165824 | tf_op jit(solution)/shard_map/heat/pallas_call | solution.py:700
  120.1 0.0 all-to-all-done.4.all_ref
  120.1 2.6 %add_source.1 = f32[16,64,512]{2,1,0:T(8,128)} custom-call(f32[32,8,128]{2,1,0:T(8,128)} %all-to-all-done.4.all_ref, f32[24,8,128]{2,1,0:T(8,128)} %get-tuple-element.88.thin_ref, f32[16,64,512]{2,1,0:T(8,128)} %get-tuple-element.89.base_ref), custom_call_target="tpu_custom_call", output_to_operand_aliasing={{}: (2, {})} | custom-call | flops 1000000 | bytes 1048576 | tf_op jit(solution)/shard_map/add_source/pallas_call | solution.py:809
Async XLA Ops:
  2.8 18.0 %all-to-all-start = ((f32[32,16,128]{2,1,0:T(8,128)}), f32[32,16,128]{2,1,0:T(8,128)}, u32[]{:S(2)}, u32[]{:S(2)}) async-start(f32[32,16,128]{2,1,0:T(8,128)} %get-tuple-element.48), calls=%async_computation | async-start | bytes 524288 | tf_op jit(solution)/shard_map/all_to_all | solution.py:827
  12.5 29.6 %collective-permute-start.2 = (f32[4,64,512]{2,1,0:T(8,128)}, f32[4,64,512]{2,1,0:T(8,128)}, u32[]{:S(2)}, u32[]{:S(2)}) collective-permute-start(f32[4,64,512]{2,1,0:T(8,128)} %get-tuple-element.90), channel_id=1, source_target_pairs={{0,4},{4,8},{8,12},{12,16},{16,20},{20,24},{24,28},{1,5},{5,9},{9,... | collective-permute-start | bytes 1572872 | tf_op jit(solution)/shard_map/ppermute | solution.py:838
  16.9 25.2 %collective-permute-start.3 = (f32[4,64,512]{2,1,0:T(8,128)}, f32[4,64,512]{2,1,0:T(8,128)}, u32[]{:S(2)}, u32[]{:S(2)}) collective-permute-start(f32[4,64,512]{2,1,0:T(8,128)} %get-tuple-element.91), channel_id=1, source_target_pairs={{4,0},{8,4},{12,8},{16,12},{20,16},{24,20},{28,24},{5,1},{9,5},{13... | collective-permute-start | bytes 1572872 | tf_op jit(solution)/shard_map/ppermute | solution.py:839
  28.0 18.5 %all-to-all-start.1 = ((f32[32,16,128]{2,1,0:T(8,128)}), f32[32,16,128]{2,1,0:T(8,128)}, u32[]{:S(2)}, u32[]{:S(2)}) async-start(f32[32,16,128]{2,1,0:T(8,128)} %bitcast.5), calls=%async_computation.1 | async-start | bytes 524288 | tf_op jit(solution)/shard_map/all_to_all | solution.py:827
  38.0 4.1 %collective-permute-start = (f32[16,8,512]{2,1,0:T(8,128)}, f32[16,8,512]{2,1,0:T(8,128)}, u32[]{:S(2)}, u32[]{:S(2)}) collective-permute-start(f32[16,8,512]{2,1,0:T(8,128)} %get-tuple-element.54), channel_id=1, source_target_pairs={{0,1},{1,2},{2,3},{4,5},{5,6},{6,7},{8,9},{9,10},{10,11},{12,13},{... | collective-permute-start | bytes 786440 | tf_op jit(solution)/shard_map/ppermute | solution.py:838
  40.7 4.2 %collective-permute-start.1 = (f32[16,8,512]{2,1,0:T(8,128)}, f32[16,8,512]{2,1,0:T(8,128)}, u32[]{:S(2)}, u32[]{:S(2)}) collective-permute-start(f32[16,8,512]{2,1,0:T(8,128)} %get-tuple-element.55), channel_id=1, source_target_pairs={{1,0},{2,1},{3,2},{5,4},{6,5},{7,6},{9,8},{10,9},{11,10},{13,12},{... | collective-permute-start | bytes 786440 | tf_op jit(solution)/shard_map/ppermute | solution.py:839
  48.2 18.1 %all-to-all-start.2 = ((f32[32,16,128]{2,1,0:T(8,128)}), f32[32,16,128]{2,1,0:T(8,128)}, u32[]{:S(2)}, u32[]{:S(2)}) async-start(f32[32,16,128]{2,1,0:T(8,128)} %middle.1), calls=%async_computation.2 | async-start | bytes 524288 | tf_op jit(solution)/shard_map/all_to_all | solution.py:827
  58.1 29.9 %collective-permute-start.5 = (f32[288,512]{1,0:T(8,128)}, f32[288,512]{1,0:T(8,128)}, u32[]{:S(2)}, u32[]{:S(2)}) collective-permute-start(f32[288,512]{1,0:T(8,128)} %get-tuple-element.63), channel_id=1, source_target_pairs={{4,0},{8,4},{12,8},{16,12},{20,16},{24,20},{28,24},{5,1},{9,5},{13... | collective-permute-start | bytes 1769480 | tf_op jit(solution)/shard_map/ppermute | solution.py:839
  59.4 32.3 %collective-permute-start.4 = (f32[288,512]{1,0:T(8,128)}, f32[288,512]{1,0:T(8,128)}, u32[]{:S(2)}, u32[]{:S(2)}) collective-permute-start(f32[288,512]{1,0:T(8,128)} %get-tuple-element.64), channel_id=1, source_target_pairs={{0,4},{4,8},{8,12},{12,16},{16,20},{20,24},{24,28},{1,5},{5,9},{9,... | collective-permute-start | bytes 1769480 | tf_op jit(solution)/shard_map/ppermute | solution.py:838
  73.6 18.3 %all-to-all-start.3 = ((f32[32,16,128]{2,1,0:T(8,128)}), f32[32,16,128]{2,1,0:T(8,128)}, u32[]{:S(2)}, u32[]{:S(2)}) async-start(f32[32,16,128]{2,1,0:T(8,128)} %bitcast.6), calls=%async_computation.3 | async-start | bytes 524288 | tf_op jit(solution)/shard_map/all_to_all | solution.py:827
  94.0 26.1 %all-to-all-start.4 = ((f32[32,8,128]{2,1,0:T(8,128)}), f32[32,8,128]{2,1,0:T(8,128)}, u32[]{:S(2)}, u32[]{:S(2)}) async-start(f32[32,8,128]{2,1,0:T(8,128)} %get-tuple-element.75), calls=%async_computation.4 | async-start | bytes 262144 | tf_op jit(solution)/shard_map/all_to_all | solution.py:827

commit v5 on v4

--- a/solution.py
+++ b/solution.py
@@ -592,7 +592,7 @@
 
 def heat_kernel(
     own_field, own_faces, own_gz, own_thin, k_low, k_high, t_low, t_high, out_ref, thin_ref,
-    loaded, corners, field, between, faces, gz, placed, sems, own_sems,
+    loaded, corners, field, between, faces, gz, placed, sems, own_sems, out_sems,
 ):
     nx, wide, nz = own_field.shape
     ny = wide - 2 * ROWS
@@ -685,10 +685,18 @@
         old, new = new, old
     one_step(old, faces, gz, HALO, tall - HALO, outside)
 
-    @pl.loop(0, nx)
-    def _(x):
-        for j, z in enumerate(spans):
-            out_ref[x, :, z] = placed[x, j, :ny, :]
+    results = [
+        pltpu.make_async_copy(
+            placed.at[:, j, pl.ds(0, ny)],
+            out_ref.at[:, :, pl.ds(j * LANES, LANES)],
+            out_sems.at[j],
+        )
+        for j in range(len(spans))
+    ]
+    for copy in results:
+        copy.start()
+    for copy in results:
+        copy.wait()
 
 
 def heat(own, k_low, k_high, t_low, t_high, shape):
@@ -704,6 +712,7 @@
             jax.ShapeDtypeStruct((tall, 8, LANES), jnp.float32),
         ),
         in_specs=[hbm] * 3 + [vmem] + [hbm] * 4,
+        out_specs=(hbm, vmem),
         scratch_shapes=[
             pltpu.VMEM((2, 2 * HALO, nz // LANES, wide, LANES), jnp.float32),
             pltpu.VMEM((2, 32, nz), jnp.float32),
@@ -714,6 +723,7 @@
             pltpu.VMEM((nx, nz // LANES, wide, LANES), jnp.float32),
             pltpu.SemaphoreType.DMA((6 * HALO, nz // LANES)),
             pltpu.SemaphoreType.DMA((5,)),
+            pltpu.SemaphoreType.DMA((nz // LANES,)),
         ],
         compiler_params=params(64),
         cost_estimate=cost(tall * wide * nz * 100, 12 * nx * ny * nz * 4),

time: 123 us -> 123 us (level); the launches traced: 123 us -> 121 us
  starting transfers between devices: 50.9 us -> 48.6 us
    all_to_all x5, starting transfers between devices: 34.5 us -> 32.2 us  [exchange(): lax.all_to_all(rows, ('slab', 'pair'), split_axis=0, concat_axis=0, tiled...]
    ppermute x3, waiting for transfers between devices: 3.67 us -> 5.85 us  [both_ways(): from_low = lax.ppermute(high, axis, forward)]
    ppermute x3, waiting for transfers between devices: 2.9 us -> 1.35 us  [both_ways(): from_high = lax.ppermute(low, axis, backward)]
  transfers between devices with their start and end apart: 11 -> 11, of which waited for: 6 -> 7; matrix products, arithmetic and copies ran while one was open for 2% -> 2% of each run, Pallas kernels for 39% -> 40%
where the time goes in v5:
time: 123 us; the launch traced here: 121 us
  Pallas kernels  56.8 us (46%)
  starting transfers between devices  48.6 us (40%)
  waiting for transfers between devices  12.5 us (10%)
  local copies, waits for them, and re-layouts  2.25 us (2%)
  between operations  1.4 us (1%)
    all_to_all x5, starting transfers between devices, exchange(): lax.all_to_all(rows, ('slab', 'pair'), split_axis=0, concat_axis=0, tiled...  32.2 us
    pallas_call x1, Pallas kernels, heat(): pl.pallas_call(heat_kernel, out_shape=(jax.ShapeDtypeStruct(shape, jnp.fl...  21.5 us
    pallas_call x2, Pallas kernels, tile_terms(): pl.pallas_call(tiles_kernel, out_shape=jax.ShapeDtypeStruct(whole.shape,...  14.4 us
    ppermute x3, starting transfers between devices, both_ways(): from_low = lax.ppermute(high, axis, forward)  12.6 us
    pallas_call x1, Pallas kernels, own_planes(): pl.pallas_call(own_planes_kernel, out_shape=(shape, shape, shape, jax.Sha...  7.93 us
    ppermute x3, waiting for transfers between devices, both_ways(): from_low = lax.ppermute(high, axis, forward)  5.85 us
    all_to_all x5, waiting for transfers between devices, exchange(): lax.all_to_all(rows, ('slab', 'pair'), split_axis=0, concat_axis=0, tiled...  5.25 us
    ppermute x3, starting transfers between devices, both_ways(): from_high = lax.ppermute(low, axis, backward)  3.84 us
  transfers between devices with their start and end apart: 11, of which 7 were waited for; matrix products, arithmetic and copies ran while one was open for 2% of the time, Pallas kernels for 40%

profile of v5, /device:TPU:0, one launch (start us, length us, event | category | flops | bytes accessed | tf_op | source)
XLA Modules:
  0.0 121.5 jit_solution(6282709636410229315)
XLA Ops:
  0.6 2.1 %emit.1 = (f32[16,128]{1,0:T(8,128)}, f32[32,16,128]{2,1,0:T(8,128)}) custom-call(f32[16,64,512]{2,1,0:T(8,128)} %t_ref, s32[16,128]{1,0:T(8,128)} %site_ref.3, f32[16,128]{1,0:T(8,128)} %mirror_ref.5), custom_call_target="tpu_custom_call" | custom-call | flops 10000 | bytes 900000 | tf_op jit(solution)/shard_map/emit/pallas_call | solution.py:96
  2.8 7.4 %all-to-all-start = ((f32[32,16,128]{2,1,0:T(8,128)}), f32[32,16,128]{2,1,0:T(8,128)}, u32[]{:S(2)}, u32[]{:S(2)}) async-start(f32[32,16,128]{2,1,0:T(8,128)} %get-tuple-element.48), calls=%async_computation | async-start | bytes 524288 | tf_op jit(solution)/shard_map/all_to_all | solution.py:837
  10.2 2.3 %fusion = (f32[4,64,512]{2,1,0:T(8,128)}, f32[4,64,512]{2,1,0:T(8,128)}) fusion(f32[16,64,512]{2,1,0:T(8,128)} %k_ref), kind=kLoop, calls=%fused_computation | loop fusion | bytes 2097152 | tf_op jit(solution)/shard_map/slice | solution.py:879
  12.5 4.4 %collective-permute-start.2 = (f32[4,64,512]{2,1,0:T(8,128)}, f32[4,64,512]{2,1,0:T(8,128)}, u32[]{:S(2)}, u32[]{:S(2)}) collective-permute-start(f32[4,64,512]{2,1,0:T(8,128)} %get-tuple-element.90), channel_id=1, source_target_pairs={{0,4},{4,8},{8,12},{12,16},{16,20},{20,24},{24,28},{1,5},{5,9},{9,... | collective-permute-start | bytes 1572872 | tf_op jit(solution)/shard_map/ppermute | solution.py:848
  16.9 1.3 %collective-permute-start.3 = (f32[4,64,512]{2,1,0:T(8,128)}, f32[4,64,512]{2,1,0:T(8,128)}, u32[]{:S(2)}, u32[]{:S(2)}) collective-permute-start(f32[4,64,512]{2,1,0:T(8,128)} %get-tuple-element.91), channel_id=1, source_target_pairs={{4,0},{8,4},{12,8},{16,12},{20,16},{24,20},{28,24},{5,1},{9,5},{13... | collective-permute-start | bytes 1572872 | tf_op jit(solution)/shard_map/ppermute | solution.py:849
  18.8 2.0 %all-to-all-done = f32[32,16,128]{2,1,0:T(8,128)} async-done(((f32[32,16,128]{2,1,0:T(8,128)}), f32[32,16,128]{2,1,0:T(8,128)}, u32[]{:S(2)}, u32[]{:S(2)}) %all-to-all-start) | async-done | bytes 262176 | tf_op jit(solution)/shard_map/all_to_all | solution.py:837
  20.8 7.2 %tiles.2 = f32[512,128]{1,0:T(8,128)} custom-call(s32[1]{0:T(128)S(6)} %copy.11.live_ref, s32[2,256]{1,0:T(2,128)} %bitcast.7, s32[2,256]{1,0:T(2,128)} %bitcast.8, f32[512,128]{1,0:T(8,128)} %bitcast.1.whole_ref, f32[256,128,128]{2,1,0:T(8,128)} %tiles_ref.3), custom_call_target="tpu_custom_call" | custom-call | flops 134217728 | bytes 16777216 | tf_op jit(solution)/shard_map/tiles/pallas_call | solution.py:200
  28.0 6.2 %all-to-all-start.1 = ((f32[32,16,128]{2,1,0:T(8,128)}), f32[32,16,128]{2,1,0:T(8,128)}, u32[]{:S(2)}, u32[]{:S(2)}) async-start(f32[32,16,128]{2,1,0:T(8,128)} %bitcast.5), calls=%async_computation.1 | async-start | bytes 524288 | tf_op jit(solution)/shard_map/all_to_all | solution.py:837
  34.2 2.0 %pack_y.1 = (f32[16,8,512]{2,1,0:T(8,128)}, f32[16,8,512]{2,1,0:T(8,128)}) custom-call(f32[16,64,512]{2,1,0:T(8,128)} %t_ref, f32[16,64,512]{2,1,0:T(8,128)} %k_ref, f32[16,64,512]{2,1,0:T(8,128)} %t_ref, f32[16,64,512]{2,1,0:T(8,128)} %k_ref), custom_call_target="tpu_custom_call" | custom-call | bytes 1048576 | tf_op jit(solution)/shard_map/pack_y/pallas_call | solution.py:297
  36.3 2.8 %collective-permute-start = (f32[16,8,512]{2,1,0:T(8,128)}, f32[16,8,512]{2,1,0:T(8,128)}, u32[]{:S(2)}, u32[]{:S(2)}) collective-permute-start(f32[16,8,512]{2,1,0:T(8,128)} %get-tuple-element.54), channel_id=1, source_target_pairs={{0,1},{1,2},{2,3},{4,5},{5,6},{6,7},{8,9},{9,10},{10,11},{12,13},{... | collective-permute-start | bytes 786440 | tf_op jit(solution)/shard_map/ppermute | solution.py:848
  39.0 1.3 %collective-permute-start.1 = (f32[16,8,512]{2,1,0:T(8,128)}, f32[16,8,512]{2,1,0:T(8,128)}, u32[]{:S(2)}, u32[]{:S(2)}) collective-permute-start(f32[16,8,512]{2,1,0:T(8,128)} %get-tuple-element.55), channel_id=1, source_target_pairs={{1,0},{2,1},{3,2},{5,4},{6,5},{7,6},{9,8},{10,9},{11,10},{13,12},{... | collective-permute-start | bytes 786440 | tf_op jit(solution)/shard_map/ppermute | solution.py:849
  40.3 1.6 %collective-permute-done.2.k_low = f32[4,64,512]{2,1,0:T(8,128)} collective-permute-done((f32[4,64,512]{2,1,0:T(8,128)}, f32[4,64,512]{2,1,0:T(8,128)}, u32[]{:S(2)}, u32[]{:S(2)}) %collective-permute-start.2) | collective-permute-done | bytes 524320 | tf_op jit(solution)/shard_map/ppermute | solution.py:848
  41.9 0.0 collective-permute-done.3.k_high
  41.9 0.0 collective-permute-done.below0.below1.below_ref
  41.9 1.3 %collective-permute-done.1.above0.above1.above_ref = f32[16,8,512]{2,1,0:T(8,128)} collective-permute-done((f32[16,8,512]{2,1,0:T(8,128)}, f32[16,8,512]{2,1,0:T(8,128)}, u32[]{:S(2)}, u32[]{:S(2)}) %collective-permute-start.1) | collective-permute-done | bytes 262176 | tf_op jit(solution)/shard_map/ppermute | solution.py:849
  43.3 1.5 %all-to-all-done.1.parts_ref = f32[32,16,128]{2,1,0:T(8,128)} async-done(((f32[32,16,128]{2,1,0:T(8,128)}), f32[32,16,128]{2,1,0:T(8,128)}, u32[]{:S(2)}, u32[]{:S(2)}) %all-to-all-start.1) | async-done | bytes 262176 | tf_op jit(solution)/shard_map/all_to_all | solution.py:837
  44.8 1.7 %middle.1 = f32[32,16,128]{2,1,0:T(8,128)} custom-call(f32[32,16,128]{2,1,0:T(8,128)} %all-to-all-done.1.parts_ref, f32[16,128]{1,0:T(8,128)} %get-tuple-element.57.emitted_ref, f32[16,128]{1,0:T(8,128)} %mirror_ref.5), custom_call_target="tpu_custom_call" | custom-call | flops 100000 | bytes 600000 | tf_op jit(solution)/shard_map/middle/pallas_call | solution.py:233
  46.5 7.6 %all-to-all-start.2 = ((f32[32,16,128]{2,1,0:T(8,128)}), f32[32,16,128]{2,1,0:T(8,128)}, u32[]{:S(2)}, u32[]{:S(2)}) async-start(f32[32,16,128]{2,1,0:T(8,128)} %middle.1), calls=%async_computation.2 | async-start | bytes 524288 | tf_op jit(solution)/shard_map/all_to_all | solution.py:837
  54.1 2.3 %pack_x.1 = (f32[288,512]{1,0:T(8,128)}, f32[288,512]{1,0:T(8,128)}) custom-call(f32[16,64,512]{2,1,0:T(8,128)} %t_ref, f32[16,64,512]{2,1,0:T(8,128)} %t_ref, f32[16,8,512]{2,1,0:T(8,128)} %collective-permute-done.below0.below1.below_ref, f32[16,8,512]{2,1,0:T(8,128)} %collective-permute-done.1.above0.above1.above_ref, ...), custom_call_target="tpu_custom_call" | custom-call | bytes 2359296 | tf_op jit(solution)/shard_map/pack_x/pallas_call | solution.py:357
  56.4 1.3 %collective-permute-start.5 = (f32[288,512]{1,0:T(8,128)}, f32[288,512]{1,0:T(8,128)}, u32[]{:S(2)}, u32[]{:S(2)}) collective-permute-start(f32[288,512]{1,0:T(8,128)} %get-tuple-element.63), channel_id=1, source_target_pairs={{4,0},{8,4},{12,8},{16,12},{20,16},{24,20},{28,24},{5,1},{9,5},{13... | collective-permute-start | bytes 1769480 | tf_op jit(solution)/shard_map/ppermute | solution.py:849
  57.7 5.4 %collective-permute-start.4 = (f32[288,512]{1,0:T(8,128)}, f32[288,512]{1,0:T(8,128)}, u32[]{:S(2)}, u32[]{:S(2)}) collective-permute-start(f32[288,512]{1,0:T(8,128)} %get-tuple-element.64), channel_id=1, source_target_pairs={{0,4},{4,8},{8,12},{12,16},{16,20},{20,24},{24,28},{1,5},{5,9},{9,... | collective-permute-start | bytes 1769480 | tf_op jit(solution)/shard_map/ppermute | solution.py:848
  63.1 1.6 %all-to-all-done.2 = f32[32,16,128]{2,1,0:T(8,128)} async-done(((f32[32,16,128]{2,1,0:T(8,128)}), f32[32,16,128]{2,1,0:T(8,128)}, u32[]{:S(2)}, u32[]{:S(2)}) %all-to-all-start.2) | async-done | bytes 262176 | tf_op jit(solution)/shard_map/all_to_all | solution.py:837
  64.7 7.2 %tiles.3 = f32[512,128]{1,0:T(8,128)} custom-call(s32[1]{0:T(128)S(6)} %copy.11.live_ref, s32[2,256]{1,0:T(2,128)} %bitcast.9, s32[2,256]{1,0:T(2,128)} %bitcast.10, f32[512,128]{1,0:T(8,128)} %bitcast.3.whole_ref, f32[256,128,128]{2,1,0:T(8,128)} %tiles_ref.3), custom_call_target="tpu_custom_call" | custom-call | flops 134217728 | bytes 16777216 | tf_op jit(solution)/shard_map/tiles/pallas_call | solution.py:200
  71.9 5.9 %all-to-all-start.3 = ((f32[32,16,128]{2,1,0:T(8,128)}), f32[32,16,128]{2,1,0:T(8,128)}, u32[]{:S(2)}, u32[]{:S(2)}) async-start(f32[32,16,128]{2,1,0:T(8,128)} %bitcast.6), calls=%async_computation.3 | async-start | bytes 524288 | tf_op jit(solution)/shard_map/all_to_all | solution.py:837
  77.8 7.9 %own_planes.1 = (f32[16,72,512]{2,1,0:T(8,128)}, f32[16,72,512]{2,1,0:T(8,128)}, f32[16,72,512]{2,1,0:T(8,128)}, f32[16,8,128]{2,1,0:T(8,128)}) custom-call(f32[16,64,512]{2,1,0:T(8,128)} %t_ref, f32[16,64,512]{2,1,0:T(8,128)} %k_ref, f32[16,8,512]{2,1,0:T(8,128)} %collective-permute-done.below0.below1.below_ref, ...), custom_call_target="tpu_custom_call" | custom-call | flops 5898240 | bytes 14155776 | tf_op jit(solution)/shard_map/own_planes/pallas_call | solution.py:579
  85.7 0.0 collective-permute-done.5.t_high
  85.7 4.3 %collective-permute-done.4.t_low = f32[288,512]{1,0:T(8,128)} collective-permute-done((f32[288,512]{1,0:T(8,128)}, f32[288,512]{1,0:T(8,128)}, u32[]{:S(2)}, u32[]{:S(2)}) %collective-permute-start.4) | collective-permute-done | bytes 589856 | tf_op jit(solution)/shard_map/ppermute | solution.py:848
  90.0 0.2 all-to-all-done.3.parts_ref
  90.1 2.2 %last.1 = (f32[16,128]{1,0:T(8,128)}, f32[32,8,128]{2,1,0:T(8,128)}) custom-call(f32[32,16,128]{2,1,0:T(8,128)} %all-to-all-done.3.parts_ref, f32[16,128]{1,0:T(8,128)} %get-tuple-element.57.emitted_ref, f32[16,128]{1,0:T(8,128)} %mirror_ref.5, s32[16,128]{1,0:T(8,128)} %site_ref.3), custom_call_target="tpu_custom_call" | custom-call | flops 10000000 | bytes 600000 | tf_op jit(solution)/shard_map/last/pallas_call | solution.py:273
  92.3 5.1 %all-to-all-start.4 = ((f32[32,8,128]{2,1,0:T(8,128)}), f32[32,8,128]{2,1,0:T(8,128)}, u32[]{:S(2)}, u32[]{:S(2)}) async-start(f32[32,8,128]{2,1,0:T(8,128)} %get-tuple-element.75), calls=%async_computation.4 | async-start | bytes 262144 | tf_op jit(solution)/shard_map/all_to_all | solution.py:837
  97.4 21.5 %heat.1 = (f32[16,64,512]{2,1,0:T(8,128)}, f32[24,8,128]{2,1,0:T(8,128)}) custom-call(f32[16,72,512]{2,1,0:T(8,128)} %get-tuple-element.80.own_field, f32[16,72,512]{2,1,0:T(8,128)} %get-tuple-element.81.own_faces, f32[16,72,512]{2,1,0:T(8,128)} %get-tuple-element.82.own_gz, f32[16,8,128]{2,1,0:T(8,128)} %get-tuple-element.83.own_thin, ...), custom_call_target="tpu_custom_call" | custom-call | flops 88473600 | bytes 25165824 | tf_op jit(solution)/shard_map/heat/pallas_call | solution.py:708
  118.9 0.0 all-to-all-done.4.all_ref
  118.9 2.6 %add_source.1 = f32[16,64,512]{2,1,0:T(8,128)} custom-call(f32[32,8,128]{2,1,0:T(8,128)} %all-to-all-done.4.all_ref, f32[24,8,128]{2,1,0:T(8,128)} %get-tuple-element.88.thin_ref, f32[16,64,512]{2,1,0:T(8,128)} %get-tuple-element.89.base_ref), custom_call_target="tpu_custom_call", output_to_operand_aliasing={{}: (2, {})} | custom-call | flops 1000000 | bytes 1048576 | tf_op jit(solution)/shard_map/add_source/pallas_call | solution.py:819
Async XLA Ops:
  2.8 18.0 %all-to-all-start = ((f32[32,16,128]{2,1,0:T(8,128)}), f32[32,16,128]{2,1,0:T(8,128)}, u32[]{:S(2)}, u32[]{:S(2)}) async-start(f32[32,16,128]{2,1,0:T(8,128)} %get-tuple-element.48), calls=%async_computation | async-start | bytes 524288 | tf_op jit(solution)/shard_map/all_to_all | solution.py:837
  12.5 29.4 %collective-permute-start.2 = (f32[4,64,512]{2,1,0:T(8,128)}, f32[4,64,512]{2,1,0:T(8,128)}, u32[]{:S(2)}, u32[]{:S(2)}) collective-permute-start(f32[4,64,512]{2,1,0:T(8,128)} %get-tuple-element.90), channel_id=1, source_target_pairs={{0,4},{4,8},{8,12},{12,16},{16,20},{20,24},{24,28},{1,5},{5,9},{9,... | collective-permute-start | bytes 1572872 | tf_op jit(solution)/shard_map/ppermute | solution.py:848
  16.9 25.0 %collective-permute-start.3 = (f32[4,64,512]{2,1,0:T(8,128)}, f32[4,64,512]{2,1,0:T(8,128)}, u32[]{:S(2)}, u32[]{:S(2)}) collective-permute-start(f32[4,64,512]{2,1,0:T(8,128)} %get-tuple-element.91), channel_id=1, source_target_pairs={{4,0},{8,4},{12,8},{16,12},{20,16},{24,20},{28,24},{5,1},{9,5},{13... | collective-permute-start | bytes 1572872 | tf_op jit(solution)/shard_map/ppermute | solution.py:849
  28.0 16.8 %all-to-all-start.1 = ((f32[32,16,128]{2,1,0:T(8,128)}), f32[32,16,128]{2,1,0:T(8,128)}, u32[]{:S(2)}, u32[]{:S(2)}) async-start(f32[32,16,128]{2,1,0:T(8,128)} %bitcast.5), calls=%async_computation.1 | async-start | bytes 524288 | tf_op jit(solution)/shard_map/all_to_all | solution.py:837
  36.3 5.6 %collective-permute-start = (f32[16,8,512]{2,1,0:T(8,128)}, f32[16,8,512]{2,1,0:T(8,128)}, u32[]{:S(2)}, u32[]{:S(2)}) collective-permute-start(f32[16,8,512]{2,1,0:T(8,128)} %get-tuple-element.54), channel_id=1, source_target_pairs={{0,1},{1,2},{2,3},{4,5},{5,6},{6,7},{8,9},{9,10},{10,11},{12,13},{... | collective-permute-start | bytes 786440 | tf_op jit(solution)/shard_map/ppermute | solution.py:848
  39.0 4.2 %collective-permute-start.1 = (f32[16,8,512]{2,1,0:T(8,128)}, f32[16,8,512]{2,1,0:T(8,128)}, u32[]{:S(2)}, u32[]{:S(2)}) collective-permute-start(f32[16,8,512]{2,1,0:T(8,128)} %get-tuple-element.55), channel_id=1, source_target_pairs={{1,0},{2,1},{3,2},{5,4},{6,5},{7,6},{9,8},{10,9},{11,10},{13,12},{... | collective-permute-start | bytes 786440 | tf_op jit(solution)/shard_map/ppermute | solution.py:849
  46.5 18.1 %all-to-all-start.2 = ((f32[32,16,128]{2,1,0:T(8,128)}), f32[32,16,128]{2,1,0:T(8,128)}, u32[]{:S(2)}, u32[]{:S(2)}) async-start(f32[32,16,128]{2,1,0:T(8,128)} %middle.1), calls=%async_computation.2 | async-start | bytes 524288 | tf_op jit(solution)/shard_map/all_to_all | solution.py:837
  56.4 29.3 %collective-permute-start.5 = (f32[288,512]{1,0:T(8,128)}, f32[288,512]{1,0:T(8,128)}, u32[]{:S(2)}, u32[]{:S(2)}) collective-permute-start(f32[288,512]{1,0:T(8,128)} %get-tuple-element.63), channel_id=1, source_target_pairs={{4,0},{8,4},{12,8},{16,12},{20,16},{24,20},{28,24},{5,1},{9,5},{13... | collective-permute-start | bytes 1769480 | tf_op jit(solution)/shard_map/ppermute | solution.py:849
  57.7 32.3 %collective-permute-start.4 = (f32[288,512]{1,0:T(8,128)}, f32[288,512]{1,0:T(8,128)}, u32[]{:S(2)}, u32[]{:S(2)}) collective-permute-start(f32[288,512]{1,0:T(8,128)} %get-tuple-element.64), channel_id=1, source_target_pairs={{0,4},{4,8},{8,12},{12,16},{16,20},{20,24},{24,28},{1,5},{5,9},{9,... | collective-permute-start | bytes 1769480 | tf_op jit(solution)/shard_map/ppermute | solution.py:848
  71.9 18.3 %all-to-all-start.3 = ((f32[32,16,128]{2,1,0:T(8,128)}), f32[32,16,128]{2,1,0:T(8,128)}, u32[]{:S(2)}, u32[]{:S(2)}) async-start(f32[32,16,128]{2,1,0:T(8,128)} %bitcast.6), calls=%async_computation.3 | async-start | bytes 524288 | tf_op jit(solution)/shard_map/all_to_all | solution.py:837
  92.3 26.6 %all-to-all-start.4 = ((f32[32,8,128]{2,1,0:T(8,128)}), f32[32,8,128]{2,1,0:T(8,128)}, u32[]{:S(2)}, u32[]{:S(2)}) async-start(f32[32,8,128]{2,1,0:T(8,128)} %get-tuple-element.75), calls=%async_computation.4 | async-start | bytes 262144 | tf_op jit(solution)/shard_map/all_to_all | solution.py:837
